TPU v7x, 128 devices: a whole 4x4x4 slice. The times are simulated.
128 devices in a mesh: expert: 64 (over z, y, x_hi, core), dp: 2 (over x_lo).
Axes of the slice: x: 4 (x_hi: 2, x_lo: 2; x = x_hi * 2 + x_lo), y: 4, z: 4, core: 2. Of those that a mesh axis runs over, the one named last changes fastest.
Arguments:
- activations: bfloat16 [16384, 3584], P(('expert', 'dp')), may hold values from -6 to 6
- out_grad: bfloat16 [16384, 3584], P(('expert', 'dp')), may hold values from -1.5 to 1.5
- expert_ids: int32 [16384, 1], P(('expert', 'dp')), may hold values from 0 to 63; in each aligned block of 128 rows (0 to 127, 128 to 255, ...) at most 6 rows name the same one
- gate_probs: bfloat16 [16384, 1], P(('expert', 'dp')), may hold values from 0.049804688 to 1
- gate_weight: bfloat16 [64, 3584, 1024], P('expert', 'dp'), may hold values from -0.09375 to 0.09375
- up_weight: bfloat16 [64, 3584, 1024], P('expert', 'dp'), may hold values from -0.09375 to 0.09375
- down_weight: bfloat16 [64, 3584, 1024], P('expert', 'dp'), may hold values from -0.1875 to 0.1875
Outputs:
- input_delta: bfloat16 [16384, 3584], P(('expert', 'dp'))
- prob_delta: bfloat16 [16384, 1], P(('expert', 'dp'))
- gate_delta: bfloat16 [64, 3584, 1024], P('expert', 'dp')
- up_delta: bfloat16 [64, 3584, 1024], P('expert', 'dp')
- down_delta: bfloat16 [64, 3584, 1024], P('expert', 'dp')
Inputs may be any that keep to these rules, and one draw needn't show every extreme that they name: `expert_ids`: among the 128 tokens of one device (aligned blocks of rows), no expert is named more than 6 times, a bound that some block reaches.
All inputs are finite; a program needn't handle non-finite values.
Results may differ from a plain program's by a relative error of at most 0.034.
Values may be sent and summed in bfloat16 or wider, within the bound.
A program may use at most 128 MiB of HBM per device.

v0:
```python
import jax
import jax.numpy as jnp
from jax import lax
from jax.sharding import PartitionSpec as P


def activate(summed, prob_rows, hidden):
    pre_gate = summed[:, :hidden]
    pre_up = summed[:, hidden : 2 * hidden]
    raw_grad = summed[:, 2 * hidden :]
    sigmoid_gate = jax.nn.sigmoid(pre_gate)
    silu_gate = pre_gate * sigmoid_gate
    hidden_rows = (silu_gate * pre_up).astype(jnp.bfloat16)
    scaled_grad = prob_rows.astype(jnp.float32)[:, None] * raw_grad
    slope = sigmoid_gate * (1.0 + pre_gate * (1.0 - sigmoid_gate))
    gate_rows = (scaled_grad * pre_up * slope).astype(jnp.bfloat16)
    up_rows = (scaled_grad * silu_gate).astype(jnp.bfloat16)
    return (hidden_rows, gate_rows, up_rows)


def on_device(activations, out_grad, expert_ids, gate_probs, gate_weight, up_weight, down_weight):
    expert_count = lax.axis_size("expert")
    group_size = lax.axis_size("dp")
    token_count = activations.shape[0]
    feature_width = activations.shape[1]
    routes_each = expert_ids.shape[1]
    capacity = max(2, 3 * token_count * routes_each // expert_count)
    slab_rows = expert_count * capacity
    group_rows = slab_rows * group_size
    w_gate = gate_weight[0]
    w_up = up_weight[0]
    w_down = down_weight[0]
    hidden = w_gate.shape[1]
    routes = expert_ids[:, 0]
    onehot = (routes[:, None] == jnp.arange(expert_count, dtype=jnp.int32)[None, :]).astype(
        jnp.int32
    )
    earlier = jnp.cumsum(onehot, axis=0) - onehot
    slot_index = jnp.sum(earlier * onehot, axis=1)
    target = routes * capacity + slot_index
    source = (
        jnp.zeros((slab_rows,), jnp.int32).at[target].set(jnp.arange(token_count, dtype=jnp.int32))
    )
    filled = jnp.zeros((slab_rows,), jnp.bool_).at[target].set(True)
    slot_probs = jnp.where(filled, gate_probs[source, 0], 0)
    send_tokens = jnp.where(filled[:, None], activations[source], 0)
    send_grads = jnp.where(filled[:, None], out_grad[source], 0)
    arrived_tokens, arrived_grads, arrived_probs = (
        lax.all_to_all(
            send_tokens.reshape(expert_count, capacity, feature_width),
            "expert",
            split_axis=0,
            concat_axis=0,
            tiled=True,
        ),
        lax.all_to_all(
            send_grads.reshape(expert_count, capacity, feature_width),
            "expert",
            split_axis=0,
            concat_axis=0,
            tiled=True,
        ),
        lax.all_to_all(
            slot_probs.reshape(expert_count, capacity),
            "expert",
            split_axis=0,
            concat_axis=0,
            tiled=True,
        ),
    )
    own_tokens = arrived_tokens.reshape(slab_rows, feature_width)
    own_grads = arrived_grads.reshape(slab_rows, feature_width)
    spread_probs = jnp.broadcast_to(arrived_probs.reshape(slab_rows, 1), (slab_rows, group_size))
    group_tokens, group_grads, group_spread = (
        lax.all_to_all(own_tokens, "dp", split_axis=1, concat_axis=0, tiled=True),
        lax.all_to_all(own_grads, "dp", split_axis=1, concat_axis=0, tiled=True),
        lax.all_to_all(spread_probs, "dp", split_axis=1, concat_axis=0, tiled=True),
    )
    group_probs = group_spread.reshape(group_rows)
    first_row = lax.axis_index("dp") * slab_rows
    own_probs = lax.dynamic_slice_in_dim(group_probs, first_row, slab_rows, 0)
    row_tokens = group_tokens
    row_grads = group_grads
    own_sums = lax.psum_scatter(
        jnp.concatenate(
            [
                jnp.dot(row_tokens, w_gate, preferred_element_type=jnp.float32),
                jnp.dot(row_tokens, w_up, preferred_element_type=jnp.float32),
                jnp.dot(row_grads, w_down, preferred_element_type=jnp.float32),
            ],
            axis=1,
        ).astype(jnp.bfloat16),
        "dp",
        scatter_dimension=0,
        tiled=True,
    ).astype(jnp.float32)
    own_hidden, gate_rows, up_rows = activate(own_sums, own_probs, hidden)
    hidden_rows = lax.all_gather(own_hidden, "dp", axis=0, tiled=True)
    accumulate_gate_rows = lax.all_gather(gate_rows, "dp", axis=0, tiled=True)
    accumulate_up_rows = lax.all_gather(up_rows, "dp", axis=0, tiled=True)
    prob_rows = lax.all_gather(own_probs, "dp", axis=0, tiled=True)
    row_tokens = group_tokens
    row_grads = group_grads
    scaled = (prob_rows.astype(jnp.float32)[:, None] * hidden_rows.astype(jnp.float32)).astype(
        jnp.bfloat16
    )
    new_gate = jnp.einsum(
        "rd,rf->df", row_tokens, accumulate_gate_rows, preferred_element_type=jnp.float32
    )
    new_up = jnp.einsum(
        "rd,rf->df", row_tokens, accumulate_up_rows, preferred_element_type=jnp.float32
    )
    new_down = jnp.einsum("rd,rf->df", row_grads, scaled, preferred_element_type=jnp.float32)
    back_rows = jnp.einsum(
        "rf,df->rd", accumulate_gate_rows, w_gate, preferred_element_type=jnp.float32
    )
    back_rows = back_rows + jnp.einsum(
        "rf,df->rd", accumulate_up_rows, w_up, preferred_element_type=jnp.float32
    )
    output_rows = jnp.einsum("rf,df->rd", hidden_rows, w_down, preferred_element_type=jnp.float32)
    inner_terms = jnp.sum(row_grads.astype(jnp.float32) * output_rows, axis=1)
    prob_terms = lax.psum_scatter(inner_terms, "dp", scatter_dimension=0, tiled=True)
    prob_rounded = prob_terms.astype(jnp.bfloat16)
    back_rounded = back_rows.astype(jnp.bfloat16)
    returned_rows = lax.all_to_all(back_rounded, "dp", split_axis=0, concat_axis=1, tiled=True)
    final_rows, final_probs = (
        lax.all_to_all(
            returned_rows.reshape(expert_count, capacity, feature_width),
            "expert",
            split_axis=0,
            concat_axis=0,
            tiled=True,
        ),
        lax.all_to_all(
            prob_rounded.reshape(expert_count, capacity),
            "expert",
            split_axis=0,
            concat_axis=0,
            tiled=True,
        ),
    )
    input_delta = final_rows.reshape(slab_rows, feature_width)[target]
    prob_delta = final_probs.reshape(slab_rows)[target][:, None]
    return (
        input_delta,
        prob_delta,
        new_gate.astype(jnp.bfloat16)[None],
        new_up.astype(jnp.bfloat16)[None],
        new_down.astype(jnp.bfloat16)[None],
    )


def solution(mesh):
    return jax.shard_map(
        on_device,
        mesh=mesh,
        in_specs=(
            P(("expert", "dp"), None),
            P(("expert", "dp"), None),
            P(("expert", "dp"), None),
            P(("expert", "dp"), None),
            P("expert", "dp", None),
            P("expert", "dp", None),
            P("expert", "dp", None),
        ),
        out_specs=(
            P(("expert", "dp"), None),
            P(("expert", "dp"), None),
            P("expert", "dp", None),
            P("expert", "dp", None),
            P("expert", "dp", None),
        ),
        check_vma=False,
    )
```

profile of v0, /device:TPU:0, one launch (start us, length us, event | category | flops | bytes accessed | tf_op | source)
XLA Modules:
  0.0 542.1 jit_solution(1405030936872476756)
XLA Ops:
  9.7 1.0 scatter_custom_fusion.1
  10.7 3.9 gather_fusion.1
  14.6 5.5 %gather.21 = bf16[64,6,3584]{2,1,0:T(8,128)(2,1)} reshape(bf16[384,3584]{1,0:T(8,128)(2,1)} %gather_fusion.1) | data formatting | bytes 5505024 | tf_op jit(solution)/shard_map/gather | solution.py:46
  20.0 3.9 gather_fusion.2
  23.9 5.4 gather.23
  29.3 1.0 scatter_custom_fusion
  30.4 4.8 broadcast_select_fusion.1
  35.3 59.4 %all_to_all.102 = bf16[64,6,3584]{2,1,0:T(8,128)(2,1)} all-to-all(bf16[64,6,3584]{2,1,0:T(8,128)(2,1)S(1)} %get-tuple-element.10), channel_id=1, replica_groups=mesh['expert'=64,'dp'=2] {'expert'}, dimensions={0} | all-to-all | bytes 5505024 | tf_op jit(solution)/shard_map/all_to_all | solution.py:49
  94.7 5.6 %all-to-all-start.4 = ((bf16[64,6,3584]{2,1,0:T(8,128)(2,1)}), bf16[64,6,3584]{2,1,0:T(8,128)(2,1)}, u32[]{:S(2)}, u32[]{:S(2)}) async-start(bf16[64,6,3584]{2,1,0:T(8,128)(2,1)} %get-tuple-element.11), calls=%async_computation.4 | async-start | bytes 7340032 | tf_op jit(solution)/shard_map/all_to_all | solution.py:56
  100.3 7.3 %all_to_all.76 = bf16[384,2,1792]{2,1,0:T(2,128)(2,1)} reshape(bf16[64,6,3584]{2,1,0:T(8,128)(2,1)} %all_to_all.102) | data formatting | bytes 5505024 | tf_op jit(solution)/shard_map/all_to_all | solution.py:75
  107.6 3.6 copy.16
  111.1 36.3 %all-to-all-done.4 = bf16[64,6,3584]{2,1,0:T(8,128)(2,1)} async-done(((bf16[64,6,3584]{2,1,0:T(8,128)(2,1)}), bf16[64,6,3584]{2,1,0:T(8,128)(2,1)}, u32[]{:S(2)}, u32[]{:S(2)}) %all-to-all-start.4) | async-done | bytes 2752544 | tf_op jit(solution)/shard_map/all_to_all | solution.py:56
  147.4 5.2 all-to-all-start.3
  152.6 7.3 %all_to_all.81 = bf16[384,2,1792]{2,1,0:T(2,128)(2,1)} reshape(bf16[64,6,3584]{2,1,0:T(8,128)(2,1)} %all-to-all-done.4) | data formatting | bytes 5505024 | tf_op jit(solution)/shard_map/all_to_all | solution.py:76
  159.9 3.6 copy.17
  163.4 22.4 %all-to-all-done.3 = bf16[384,2,1792]{2,0,1:T(8,128)(2,1)} async-done(((bf16[384,2,1792]{2,0,1:T(8,128)(2,1)}), bf16[384,2,1792]{2,0,1:T(8,128)(2,1)}, u32[]{:S(2)}, u32[]{:S(2)}) %all-to-all-start.3) | async-done | bytes 2752544 | tf_op jit(solution)/shard_map/all_to_all | solution.py:75
  185.9 5.1 all-to-all-start.5
  191.3 6.0 %fusion.16 = bf16[768,1024]{1,0:T(8,128)(2,1)S(1)} fusion(bf16[768,1792]{1,0:T(8,128)(2,1)} %bitcast.5, bf16[1,1792,1024]{2,1,0:T(8,128)(2,1)} %param.11), kind=kOutput, calls=%fused_computation.30 | convolution fusion | flops 2819358720 | bytes 7995392 | tf_op jit(solution)/shard_map/dot_general | solution.py:87
  197.3 5.9 %fusion.19 = bf16[768,1024]{1,0:T(8,128)(2,1)} fusion(bf16[768,1792]{1,0:T(8,128)(2,1)} %bitcast.5, bf16[1,1792,1024]{2,1,0:T(8,128)(2,1)S(1)} %copy-done.5), kind=kOutput, calls=%fused_computation.31 | convolution fusion | flops 2819358720 | bytes 7995392 | tf_op jit(solution)/shard_map/dot_general | solution.py:88
  203.2 18.4 %all-to-all-done.5 = bf16[384,2,1792]{2,0,1:T(8,128)(2,1)} async-done(((bf16[384,2,1792]{2,0,1:T(8,128)(2,1)}), bf16[384,2,1792]{2,0,1:T(8,128)(2,1)}, u32[]{:S(2)}, u32[]{:S(2)}) %all-to-all-start.5) | async-done | bytes 2752544 | tf_op jit(solution)/shard_map/all_to_all | solution.py:76
  221.6 6.0 %fusion.22 = bf16[768,1024]{1,0:T(8,128)(2,1)S(1)} fusion(bf16[768,1792]{1,0:T(8,128)(2,1)} %bitcast.10, bf16[1,1792,1024]{2,1,0:T(8,128)(2,1)} %param.13), kind=kOutput, calls=%fused_computation.32 | convolution fusion | flops 2819358720 | bytes 7995392 | tf_op jit(solution)/shard_map/dot_general | solution.py:89
  227.6 2.3 pad_maximum_fusion
  230.6 2.7 gather_fusion
  233.4 20.8 %all_to_all.103 = bf16[64,1,6]{2,1,0:T(2,128)(2,1)S(1)} all-to-all(bf16[64,1,6]{2,1,0:T(2,128)(2,1)S(1)} %all_to_all.91), channel_id=1, replica_groups=mesh['expert'=64,'dp'=2] {'expert'}, dimensions={0} | all-to-all | bytes 1536 | tf_op jit(solution)/shard_map/all_to_all | solution.py:63
  256.4 3.2 all-to-all-start.1
  259.7 3.7 all-to-all-done.1
  263.6 31.7 %reduce-scatter.2.cloned.1.call-done = bf16[384,3072]{1,0:T(8,128)(2,1)} async-done(((bf16[768,3072]{1,0:T(8,128)(2,1)}), bf16[384,3072]{1,0:T(8,128)(2,1)}) %reduce-scatter.2.cloned.1.call-update) | async-done | bytes 2359312 | tf_op jit(solution)/shard_map/reduce_scatter | solution.py:84
  295.3 2.2 convert_element_type.53
  297.5 2.5 multiply_convert_fusion.4
  301.4 29.5 %all-gather.7.cloned.1.call-done = bf16[768,1024]{1,0:T(8,128)(2,1)} async-done(((bf16[384,1024]{1,0:T(8,128)(2,1)}), bf16[768,1024]{1,0:T(8,128)(2,1)}) %all-gather.7.cloned.1.call-update) | async-done | bytes 1572880 | tf_op jit(solution)/shard_map/all_gather | solution.py:100
  330.9 8.0 %fusion.3 = f32[768,1792]{1,0:T(8,128)} fusion(bf16[768,1024]{1,0:T(8,128)(2,1)} %all-gather.7.cloned.1.call-done, bf16[1,1792,1024]{2,1,0:T(8,128)(2,1)} %param.12), kind=kOutput, calls=%fused_computation.16 | convolution fusion | flops 2818572288 | bytes 10747904 | tf_op jit(solution)/shard_map/rf,df->rd/dot_general | solution.py:117
  338.8 25.1 %all-gather.5.cloned.1.call-done = bf16[768,1024]{1,0:T(8,128)(2,1)} async-done(((bf16[384,1024]{1,0:T(8,128)(2,1)}), bf16[768,1024]{1,0:T(8,128)(2,1)}) %all-gather.5.cloned.1.call-update) | async-done | bytes 1572880 | tf_op jit(solution)/shard_map/all_gather | solution.py:99
  363.9 8.7 %add_convert_fusion = bf16[768,1792]{1,0:T(8,128)(2,1)} fusion(f32[768,1792]{1,0:T(8,128)} %fusion.3, bf16[768,1024]{1,0:T(8,128)(2,1)} %all-gather.5.cloned.1.call-done, bf16[1,1792,1024]{2,1,0:T(8,128)(2,1)} %param.11), kind=kOutput, calls=%fused_computation.8 | convolution fusion | flops 2821324800 | bytes 13500416 | tf_op jit(solution)/shard_map/rf,df->rd/dot_general | solution.py:114
  372.7 5.3 all-to-all-start.6
  379.2 33.7 %all-gather.9.cloned.1.call-done = bf16[768,1024]{1,0:T(8,128)(2,1)} async-done(((bf16[384,1024]{1,0:T(8,128)(2,1)}), bf16[768,1024]{1,0:T(8,128)(2,1)}) %all-gather.9.cloned.1.call-update) | async-done | bytes 1572880 | tf_op jit(solution)/shard_map/all_gather | solution.py:98
  412.9 6.5 %multiply_reduce_fusion = f32[768]{0:T(1024)S(1)} fusion(bf16[768,1792]{1,0:T(8,128)(2,1)} %bitcast.10, bf16[768,1024]{1,0:T(8,128)(2,1)} %all-gather.9.cloned.1.call-done, bf16[1,1792,1024]{2,1,0:T(8,128)(2,1)} %param.13), kind=kOutput, calls=%fused_computation.7 | convolution fusion | flops 2822700288 | bytes 7998464 | tf_op jit(solution)/shard_map/rf,df->rd/dot_general | solution.py:120
  419.4 6.8 %all-reduce.1 = bf16[768]{0:T(1024)(128)(2,1)S(1)} all-reduce(f32[768]{0:T(1024)S(1)} %multiply_reduce_fusion), channel_id=3, replica_groups=mesh['expert'=64,'dp'=2] {'dp'}, use_global_device_ids=true, to_apply=%region_6.7.clone | all-reduce | flops 768 | bytes 4608
  427.1 10.2 %all-to-all-start.8 = ((bf16[64,1,6]{2,1,0:T(2,128)(2,1)}), bf16[64,1,6]{2,1,0:T(2,128)(2,1)S(1)}, u32[]{:S(2)}, u32[]{:S(2)}) async-start(bf16[64,1,6]{2,1,0:T(2,128)(2,1)} %all_to_all.92), calls=%async_computation.9 | async-start | bytes 65536 | tf_op jit(solution)/shard_map/all_to_all | solution.py:134
  437.3 6.1 %copy.18 = bf16[384,2,1792]{2,1,0:T(2,128)(2,1)} copy(bf16[384,2,1792]{2,0,1:T(8,128)(2,1)} %bitcast.13) | data formatting | bytes 5505024 | tf_op jit(solution)/shard_map/all_to_all | solution.py:125
  443.4 7.6 %reshape.76 = bf16[64,6,3584]{2,1,0:T(8,128)(2,1)} reshape(bf16[384,2,1792]{2,1,0:T(2,128)(2,1)} %copy.18) | data formatting | bytes 5505024 | tf_op jit(solution)/shard_map/reshape | solution.py:128
  451.0 10.8 %all-to-all-start.7 = ((bf16[64,6,3584]{2,1,0:T(8,128)(2,1)}), bf16[64,6,3584]{2,1,0:T(8,128)(2,1)}, u32[]{:S(2)}, u32[]{:S(2)}) async-start(bf16[64,6,3584]{2,1,0:T(8,128)(2,1)} %reshape.76), calls=%async_computation.8 | async-start | bytes 7340032 | tf_op jit(solution)/shard_map/all_to_all | solution.py:127
  461.9 41.5 %all-gather = bf16[2,1,384]{2,1,0:T(2,128)(2,1)S(1)} all-gather(bf16[1,1,384]{2,1,0:T(2,128)(2,1)S(1)} %reshape.141), channel_id=1, replica_groups=mesh['expert'=64,'dp'=2] {'dp'}, dimensions={0}, use_global_device_ids=true | all-gather | bytes 2304 | tf_op jit(solution)/shard_map/all_gather | solution.py:101
  503.4 6.4 %fusion.12 = bf16[1,1792,1024]{2,1,0:T(8,128)(2,1)} fusion(bf16[768,1792]{1,0:T(8,128)(2,1)} %bitcast.5, bf16[768,1024]{1,0:T(8,128)(2,1)S(1)} %copy-done.6), kind=kOutput, calls=%fused_computation.27 | convolution fusion | flops 2820407296 | bytes 7995392 | tf_op jit(solution)/shard_map/rd,rf->df/dot_general | solution.py:110
  509.8 6.4 %fusion.11 = bf16[1,1792,1024]{2,1,0:T(8,128)(2,1)} fusion(bf16[768,1792]{1,0:T(8,128)(2,1)} %bitcast.5, bf16[768,1024]{1,0:T(8,128)(2,1)S(1)} %copy-done.7), kind=kOutput, calls=%fused_computation.26 | convolution fusion | flops 2820407296 | bytes 7995392 | tf_op jit(solution)/shard_map/rd,rf->df/dot_general | solution.py:107
  516.2 6.4 %fusion.13 = bf16[1,1792,1024]{2,1,0:T(8,128)(2,1)} fusion(bf16[768,1792]{1,0:T(8,128)(2,1)} %bitcast.10, bf16[768,1024]{1,0:T(8,128)(2,1)S(1)} %copy-done.8, f32[768]{0:T(1024)S(1)} %reshape.143), kind=kOutput, calls=%fused_computation.28 | convolution fusion | flops 2822766592 | bytes 7998464 | tf_op jit(solution)/shard_map/rd,rf->df/dot_general | solution.py:113
  522.9 1.8 gather_fusion.4
  524.6 5.6 %reshape.77 = bf16[384,3584]{1,0:T(8,128)(2,1)} reshape(bf16[64,6,3584]{2,1,0:T(8,128)(2,1)} %all-to-all-done.7) | data formatting | bytes 5505024 | tf_op jit(solution)/shard_map/reshape | solution.py:142
  530.2 5.1 gather_fusion.3
  (61 shorter events, 9.2 us)
Async XLA Ops:
  7.2 3.5 copy-start
  14.6 5.5 %copy-start.3 = (bf16[128,3584]{1,0:T(8,128)(2,1)S(1)}, bf16[128,3584]{1,0:T(8,128)(2,1)}, u32[]{:S(2)}) copy-start(bf16[128,3584]{1,0:T(8,128)(2,1)} %param.8) | copy-start | bytes 2752516
  94.7 52.8 %all-to-all-start.4 = ((bf16[64,6,3584]{2,1,0:T(8,128)(2,1)}), bf16[64,6,3584]{2,1,0:T(8,128)(2,1)}, u32[]{:S(2)}, u32[]{:S(2)}) async-start(bf16[64,6,3584]{2,1,0:T(8,128)(2,1)} %get-tuple-element.11), calls=%async_computation.4 | async-start | bytes 7340032 | tf_op jit(solution)/shard_map/all_to_all | solution.py:56
  147.4 38.4 %all-to-all-start.3 = ((bf16[384,2,1792]{2,0,1:T(8,128)(2,1)}), bf16[384,2,1792]{2,0,1:T(8,128)(2,1)}, u32[]{:S(2)}, u32[]{:S(2)}) async-start(bf16[384,2,1792]{2,0,1:T(8,128)(2,1)} %copy.16), calls=%async_computation.3 | async-start | bytes 5505024 | tf_op jit(solution)/shard_map/all_to_all | solution.py:75
  185.9 35.8 %all-to-all-start.5 = ((bf16[384,2,1792]{2,0,1:T(8,128)(2,1)}), bf16[384,2,1792]{2,0,1:T(8,128)(2,1)}, u32[]{:S(2)}, u32[]{:S(2)}) async-start(bf16[384,2,1792]{2,0,1:T(8,128)(2,1)} %copy.17), calls=%async_computation.5 | async-start | bytes 5505024 | tf_op jit(solution)/shard_map/all_to_all | solution.py:76
  190.9 104.4 %reduce-scatter.2.cloned.1.call-start = ((), (), s32[]{:S(2)}) async-start(), calls=%async_computation.10 | async-start | bytes 7077888 | tf_op jit(solution)/shard_map/reduce_scatter | solution.py:84
  191.3 6.0 %copy-start.5 = (bf16[1,1792,1024]{2,1,0:T(8,128)(2,1)S(1)}, bf16[1,1792,1024]{2,1,0:T(8,128)(2,1)}, u32[]{:S(2)}) copy-start(bf16[1,1792,1024]{2,1,0:T(8,128)(2,1)} %param.12) | copy-start | bytes 11010052
  221.6 6.0 %copy-start.4 = (bf16[768,1024]{1,0:T(8,128)(2,1)S(1)}, bf16[768,1024]{1,0:T(8,128)(2,1)}, u32[]{:S(2)}) copy-start(bf16[768,1024]{1,0:T(8,128)(2,1)} %fusion.19) | copy-start | bytes 4718596
  229.9 0.7 copy-start.2
  256.4 7.0 %all-to-all-start.1 = ((bf16[2,2,192]{2,1,0:T(2,128)(2,1)}), bf16[2,2,192]{2,1,0:T(2,128)(2,1)S(1)}, u32[]{:S(2)}, u32[]{:S(2)}) async-start(bf16[2,2,192]{2,1,0:T(2,128)(2,1)} %reshape.153), calls=%async_computation.1 | async-start | bytes 4096 | tf_op jit(solution)/shard_map/all_to_all | solution.py:77
  259.6 71.3 %all-gather.7.cloned.1.call-start = ((), (), s32[]{:S(2)}) async-start(), calls=%async_computation.12 | async-start | bytes 2359296 | tf_op jit(solution)/shard_map/all_gather | solution.py:100
  300.0 63.9 %all-gather.5.cloned.1.call-start = ((), (), s32[]{:S(2)}) async-start(), calls=%async_computation.11 | async-start | bytes 2359296 | tf_op jit(solution)/shard_map/all_gather | solution.py:99
  300.8 112.2 %all-gather.9.cloned.1.call-start = ((), (), s32[]{:S(2)}) async-start(), calls=%async_computation.13 | async-start | bytes 2359296 | tf_op jit(solution)/shard_map/all_gather | solution.py:98
  372.7 5.3 copy-start.9
  372.7 54.4 %all-to-all-start.6 = ((bf16[2,384,1792]{2,1,0:T(8,128)(2,1)}), bf16[2,384,1792]{2,1,0:T(8,128)(2,1)}, u32[]{:S(2)}, u32[]{:S(2)}) async-start(bf16[2,384,1792]{2,1,0:T(8,128)(2,1)} %bitcast.63), calls=%async_computation.7 | async-start | bytes 5505024 | tf_op jit(solution)/shard_map/all_to_all | solution.py:125
  427.1 23.9 %all-to-all-start.8 = ((bf16[64,1,6]{2,1,0:T(2,128)(2,1)}), bf16[64,1,6]{2,1,0:T(2,128)(2,1)S(1)}, u32[]{:S(2)}, u32[]{:S(2)}) async-start(bf16[64,1,6]{2,1,0:T(2,128)(2,1)} %all_to_all.92), calls=%async_computation.9 | async-start | bytes 65536 | tf_op jit(solution)/shard_map/all_to_all | solution.py:134
  451.0 52.3 %copy-start.6 = (bf16[768,1024]{1,0:T(8,128)(2,1)S(1)}, bf16[768,1024]{1,0:T(8,128)(2,1)}, u32[]{:S(2)}) copy-start(bf16[768,1024]{1,0:T(8,128)(2,1)} %all-gather.7.cloned.1.call-done) | copy-start | bytes 4718596
  451.0 73.6 %all-to-all-start.7 = ((bf16[64,6,3584]{2,1,0:T(8,128)(2,1)}), bf16[64,6,3584]{2,1,0:T(8,128)(2,1)}, u32[]{:S(2)}, u32[]{:S(2)}) async-start(bf16[64,6,3584]{2,1,0:T(8,128)(2,1)} %reshape.76), calls=%async_computation.8 | async-start | bytes 7340032 | tf_op jit(solution)/shard_map/all_to_all | solution.py:127
  503.4 6.4 %copy-start.7 = (bf16[768,1024]{1,0:T(8,128)(2,1)S(1)}, bf16[768,1024]{1,0:T(8,128)(2,1)}, u32[]{:S(2)}) copy-start(bf16[768,1024]{1,0:T(8,128)(2,1)} %all-gather.5.cloned.1.call-done) | copy-start | bytes 4718596
  509.8 6.4 %copy-start.8 = (bf16[768,1024]{1,0:T(8,128)(2,1)S(1)}, bf16[768,1024]{1,0:T(8,128)(2,1)}, u32[]{:S(2)}) copy-start(bf16[768,1024]{1,0:T(8,128)(2,1)} %all-gather.9.cloned.1.call-done) | copy-start | bytes 4718596
  524.6 10.7 %copy-start.1 = (bf16[128,3584]{1,0:T(8,128)(2,1)S(1)}, bf16[128,3584]{1,0:T(8,128)(2,1)}, u32[]{:S(2)}) copy-start(bf16[128,3584]{1,0:T(8,128)(2,1)} %param.7) | copy-start | bytes 2752516
Sparse Core Ops, SparseCore 0:
  230.1 65.1 reduce-scatter.1
  300.1 30.6 all-gather.6
  333.2 30.6 all-gather.4
  366.1 46.7 all-gather.8
where the time goes:
time: 553 us; the launch traced here: 542 us
  waiting for transfers between devices  202 us (37%)
  blocking collectives  128 us (23%)
  local copies, waits for them, and re-layouts  75.1 us (14%)
  matrix products  60.3 us (11%)
  starting transfers between devices  46.3 us (8%)
  other arithmetic  15.3 us (3%)
  between operations  14.9 us (3%)
    all_to_all x1, blocking collectives, on_device(): lax.all_to_all(send_tokens.reshape(expert_count, capacity, feature_width)...  59.4 us
    all_gather x1, blocking collectives, on_device(): prob_rows = lax.all_gather(own_probs, 'dp', axis=0, tiled=True)  41.5 us
    all_to_all x1, waiting for transfers between devices, on_device(): lax.all_to_all(send_grads.reshape(expert_count, capacity, feature_width),...  36.3 us
    all_gather x1, waiting for transfers between devices, on_device(): hidden_rows = lax.all_gather(own_hidden, 'dp', axis=0, tiled=True)  33.7 us
    reduce_scatter x1, waiting for transfers between devices, on_device(): lax.psum_scatter(jnp.concatenate([jnp.dot(row_tokens, w_gate, preferred_e...  31.7 us
    all_gather x1, waiting for transfers between devices, on_device(): accumulate_up_rows = lax.all_gather(up_rows, 'dp', axis=0, tiled=True)  29.5 us
    all_gather x1, waiting for transfers between devices, on_device(): accumulate_gate_rows = lax.all_gather(gate_rows, 'dp', axis=0, tiled=True)  25.1 us
    all_to_all x1, waiting for transfers between devices, on_device(): lax.all_to_all(own_tokens, 'dp', split_axis=1, concat_axis=0, tiled=True)  22.4 us
  transfers between devices with their start and end apart: 11, of which 8 were waited for; matrix products, arithmetic and copies ran while one was open for 15% of the time, Pallas kernels for 0%

commit v1 on v0

v1 whole, which is shorter than its diff:
```python
import functools

import jax
import jax.numpy as jnp
from jax import lax
from jax.experimental import pallas as pl
from jax.experimental.pallas import tpu as pltpu
from jax.sharding import PartitionSpec as P

MESH = pl.DeviceIdType.MESH
BF = jnp.bfloat16
F32 = jnp.float32
TOK = 128
CAP = 6
SLAB = 4 * CAP
GROUP = 8
ROWS = GROUP * SLAB
WIDE = 1792
HID = 1024
EXTRA = 128
TILE = 256


def rem(a, b):
    return lax.rem(a, jnp.int32(b))


def div(a, b):
    return lax.div(a, jnp.int32(b))


def dot(a, b, dims):
    return lax.dot_general(a, b, ((dims[:1], dims[1:]), ((), ())), preferred_element_type=F32)


def kernel(
    ids_col, ids_row, p_row, p_col, x, g, wg, wu, wd,
    dx, dprob, gg, gu, gd,
    vw, meta, xr, gr, one, onep, onet, sx, sg, x3, g3,
    pgu, pr, qgu, qr, rows_gu, rows_h, b3, r3, out_s, out_r,
    w_sem, m_send, m_recv, x_send, x_recv, y_send, y_recv, d_send, d_recv,
    b_send, b_recv, o_send, o_recv, g_sem,
):
    e = lax.axis_index("expert")
    xl = lax.axis_index("dp")
    core, xh, y, z = rem(e, 2), rem(div(e, 2), 2), rem(div(e, 4), 4), div(e, 16)
    mine = xh * 2 + xl
    own_slab = div(e, 4) * 2 + core

    def mate(i):
        th, tl = rem(xh + i // 2, 2), rem(xl + i % 2, 2)
        return th, tl, th * 2 + tl, (div(e, 4) * 4 + th * 2 + core, tl)

    def plane(q, sign):
        dz = rem(div(q * (q + 1), 2), 4)
        return rem(z + dz if sign > 0 else z + 4 - dz, 4)

    def half(ref, k):
        return ref.at[:, pl.ds(pl.multiple_of(k * WIDE, WIDE), WIDE)]

    def part(ref, m):
        return ref.at[pl.ds(pl.multiple_of(m * TOK, TOK), TOK)]

    for i, w in enumerate((wg, wu, wd)):
        pltpu.make_async_copy(w.at[0], vw.at[i], w_sem.at[i]).start()

    def x_copy(a, src, dst, i):
        _, tl, m, where = mate(i)
        return pltpu.make_async_remote_copy(
            src_ref=half(src, tl), dst_ref=part(dst, mine),
            send_sem=x_send.at[a, i], recv_sem=x_recv.at[a, i],
            device_id=where, device_id_type=MESH,
        )

    def x_own(a, src, dst):
        return pltpu.make_async_copy(half(src, xl), part(dst, mine), x_recv.at[a, 0])

    for i in (2, 1, 3):
        x_copy(0, x, xr, i).start()
    x_own(0, x, xr).start()

    ids = ids_row[...]
    before = lax.broadcasted_iota(jnp.int32, (TOK, TOK), 0) < lax.broadcasted_iota(
        jnp.int32, (TOK, TOK), 1
    )
    same = jnp.where((ids_col[...] == ids) & before, 1.0, 0.0)
    rank = jnp.sum(same, axis=0, keepdims=True)
    side = ((ids >> 1) & 1).astype(F32)
    row = ((ids >> 2) * 2 + (ids & 1)) * SLAB + mine * CAP
    meta[mine, 0:1, :] = side
    meta[mine, 1:2, :] = row.astype(F32) + rank
    meta[mine, 2:3, :] = p_row[...]
    meta[mine, 3:8, :] = jnp.zeros((5, TOK), F32)

    def m_copy(i):
        return pltpu.make_async_remote_copy(
            src_ref=meta.at[mine], dst_ref=meta.at[mine],
            send_sem=m_send.at[i], recv_sem=m_recv.at[i],
            device_id=mate(i)[3], device_id_type=MESH,
        )

    for i in (2, 1, 3):
        m_copy(i).start()
    for i in (2, 1, 3):
        x_copy(1, g, gr, i).start()
    x_own(1, g, gr).start()

    for i in (1, 2, 3):
        m_copy(i).wait_recv()
    my_side = xh.astype(F32)
    for m in range(4):
        want = jnp.where(meta[m, 0:1, :] == my_side, meta[m, 1:2, :], -1.0)
        prob = meta[m, 2:3, :]
        for r in range(4):
            at = lax.broadcasted_iota(jnp.int32, (ROWS, TOK), 0).astype(F32) + float(r * ROWS)
            hit = at == want
            one[r * ROWS : (r + 1) * ROWS, m * TOK : (m + 1) * TOK] = jnp.where(
                hit, 1.0, 0.0
            ).astype(BF)
            onep[r * ROWS : (r + 1) * ROWS, m * TOK : (m + 1) * TOK] = jnp.where(
                hit, prob, 0.0
            ).astype(BF)
        down = jnp.transpose(jnp.broadcast_to(want, (TOK, TOK)))
        for r in range(4 * ROWS // TOK):
            at = lax.broadcasted_iota(jnp.int32, (TOK, TOK), 1).astype(F32) + float(r * TOK)
            onet[m * TOK : (m + 1) * TOK, r * TOK : (r + 1) * TOK] = jnp.where(
                at == down, 1.0, 0.0
            ).astype(BF)

    def group_send(q, sign, src, dst, s_sem, r_sem):
        zt = plane(q, sign)

        def one_send(i, _):
            yt, ct = rem(y + div(i, 2), 4), rem(core + rem(i, 2), 2)
            pltpu.make_async_remote_copy(
                src_ref=src.at[(zt * 4 + yt) * 2 + ct], dst_ref=dst.at[own_slab],
                send_sem=s_sem, recv_sem=r_sem,
                device_id=(((zt * 4 + yt) * 2 + xh) * 2 + ct, xl), device_id_type=MESH,
            ).start()
            return 0

        first = jnp.where(q == 0, 1, 0).astype(jnp.int32) if not isinstance(q, int) else int(q == 0)
        lax.fori_loop(first, GROUP, one_send, 0)

    def group_wait(count, first, src, dst, sem):
        pltpu.make_async_copy(
            src.at[pl.ds(first, count)], dst.at[pl.ds(first, count)], sem
        ).wait()

    def gather_and_send(a, picks, rows, src, dst):
        for q in range(4):
            zt = plane(jnp.int32(q), 1)

            @pl.loop(0, WIDE // TILE)
            def _(n):
                lanes = pl.ds(pl.multiple_of(n * TILE, TILE), TILE)
                got = dot(picks[pl.ds(pl.multiple_of(zt * ROWS, ROWS), ROWS), :], rows[:, lanes], (1, 0))
                src[pl.ds(zt * GROUP, GROUP), :, lanes] = got.astype(BF).reshape(GROUP, SLAB, TILE)

            group_send(q, 1, src, dst, y_send.at[a, q], y_recv.at[a, q])
            if q == 0:
                pltpu.make_async_copy(src.at[own_slab], dst.at[own_slab], y_recv.at[a, 0]).start()

    for i in (1, 2, 3):
        x_copy(0, x, xr, i).wait_recv()
    x_own(0, x, xr).wait()
    gather_and_send(0, one, xr, sx, x3)
    for i in (1, 2, 3):
        x_copy(1, g, gr, i).wait_recv()
    x_own(1, g, gr).wait()
    gather_and_send(1, onep, gr, sg, g3)

    other = (e, 1 - xl)

    def d_copy(a, q):
        src, dst = ((pgu, qgu), (pr, qr))[a]
        at = plane(q, -1)
        return pltpu.make_async_remote_copy(
            src_ref=src.at[at], dst_ref=dst.at[at],
            send_sem=d_send.at[a, q], recv_sem=d_recv.at[a, q],
            device_id=other, device_id_type=MESH,
        )

    for i, w in enumerate((wg, wu, wd)):
        pltpu.make_async_copy(w.at[0], vw.at[i], w_sem.at[i]).wait()

    @pl.loop(0, 4)
    def _(q):
        at = plane(q, -1)
        group_wait(GROUP, at * GROUP, sx, x3, y_recv.at[0, q])

        @pl.loop(0, HID // TILE)
        def _(n):
            lanes = pl.ds(pl.multiple_of(n * TILE, TILE), TILE)
            more = pl.ds(pl.multiple_of(HID + n * TILE, TILE), TILE)
            left = x3[pl.ds(at * GROUP, GROUP)].reshape(ROWS, WIDE)
            pgu[at, :, lanes] = dot(left, vw[0, :, lanes], (1, 0)).astype(BF)
            pgu[at, :, more] = dot(left, vw[1, :, lanes], (1, 0)).astype(BF)

        d_copy(0, q).start()

    @pl.loop(0, 4)
    def _(q):
        at = plane(q, -1)
        group_wait(GROUP, at * GROUP, sg, g3, y_recv.at[1, q])

        @pl.loop(0, HID // TILE)
        def _(n):
            lanes = pl.ds(pl.multiple_of(n * TILE, TILE), TILE)
            left = g3[pl.ds(at * GROUP, GROUP)].reshape(ROWS, WIDE)
            pr[at, :, lanes] = dot(left, vw[2, :, lanes], (1, 0)).astype(BF)

        d_copy(1, q).start()

    for q in range(4):
        at = plane(jnp.int32(q), -1)
        d_copy(0, jnp.int32(q)).wait_recv()
        d_copy(1, jnp.int32(q)).wait_recv()
        here = pl.ds(pl.multiple_of(at * ROWS, ROWS), ROWS)

        def act(n, total):
            lanes = pl.ds(pl.multiple_of(n * TILE, TILE), TILE)
            more = pl.ds(pl.multiple_of(HID + n * TILE, TILE), TILE)
            gate = pgu[at, :, lanes].astype(F32) + qgu[at, :, lanes].astype(F32)
            up = pgu[at, :, more].astype(F32) + qgu[at, :, more].astype(F32)
            d = pr[at, :, lanes].astype(F32) + qr[at, :, lanes].astype(F32)
            s = jax.nn.sigmoid(gate)
            silu = gate * s
            hidden = silu * up
            rows_h[here, lanes] = hidden.astype(BF)
            rows_gu[here, lanes] = (d * up * (s * (1.0 + gate * (1.0 - s)))).astype(BF)
            rows_gu[here, more] = (d * silu).astype(BF)
            return total + jnp.sum(hidden * d, axis=1, keepdims=True)

        total = lax.fori_loop(0, HID // TILE, act, jnp.zeros((ROWS, 1), F32))
        b3[pl.ds(at * GROUP, GROUP), :, WIDE:] = (
            jnp.broadcast_to(total, (ROWS, EXTRA)).astype(BF).reshape(GROUP, SLAB, EXTRA)
        )

        @pl.loop(0, WIDE // TILE)
        def _(n):
            lanes = pl.ds(pl.multiple_of(n * TILE, TILE), TILE)
            back = dot(rows_gu[here, :HID], vw[0, lanes, :], (1, 1)) + dot(
                rows_gu[here, HID:], vw[1, lanes, :], (1, 1)
            )
            b3[pl.ds(at * GROUP, GROUP), :, lanes] = back.astype(BF).reshape(GROUP, SLAB, TILE)

        group_send(q, -1, b3, r3, b_send.at[q], b_recv.at[q])
        if q == 0:
            pltpu.make_async_copy(b3.at[own_slab], r3.at[own_slab], b_recv.at[0]).start()

    def g_copy(i, n):
        rows = pl.ds(pl.multiple_of(n * TILE, TILE), TILE)
        return pltpu.make_async_copy(vw.at[i, rows], (gg, gu, gd)[i].at[0, rows], g_sem.at[i, n])

    @pl.loop(0, WIDE // TILE)
    def _(n):
        lanes = pl.ds(pl.multiple_of(n * TILE, TILE), TILE)
        left = x3[:, :, lanes].reshape(4 * ROWS, TILE)
        vw[0, lanes, :] = dot(left, rows_gu[:, :HID], (0, 0)).astype(BF)
        vw[1, lanes, :] = dot(left, rows_gu[:, HID:], (0, 0)).astype(BF)
        g_copy(0, n).start()
        g_copy(1, n).start()

    for q in range(4):
        group_wait(GROUP, plane(jnp.int32(q), 1) * GROUP, b3, r3, b_recv.at[q])

    def pick(m):
        return dot(
            onet[pl.ds(pl.multiple_of(m * TOK, TOK), TOK), :],
            r3[...].reshape(4 * ROWS, WIDE + EXTRA), (1, 0),
        ).astype(BF)

    def o_copy(i):
        _, _, m, where = mate(i)
        return pltpu.make_async_remote_copy(
            src_ref=out_s.at[m], dst_ref=out_r.at[mine],
            send_sem=o_send.at[i], recv_sem=o_recv.at[i],
            device_id=where, device_id_type=MESH,
        )

    for i in (2, 1, 3):
        m = mate(i)[2]
        out_s[m] = pick(m)
        o_copy(i).start()
    out_r[mine] = pick(mine)

    @pl.loop(0, WIDE // TILE)
    def _(n):
        lanes = pl.ds(pl.multiple_of(n * TILE, TILE), TILE)
        left = g3[:, :, lanes].reshape(4 * ROWS, TILE)
        vw[2, lanes, :] = dot(left, rows_h[...], (0, 0)).astype(BF)
        g_copy(2, n).start()

    for i in (1, 2, 3):
        o_copy(i).wait_recv()
    for k in range(2):
        dx[:, k * WIDE : (k + 1) * WIDE] = (
            out_r[k, :, :WIDE].astype(F32) + out_r[2 + k, :, :WIDE].astype(F32)
        ).astype(BF)
    term = out_r[0, :, WIDE : WIDE + 1].astype(F32) + out_r[2, :, WIDE : WIDE + 1].astype(F32)
    dprob[...] = (term / p_col[...].astype(F32)).astype(BF)

    for i in (1, 2, 3):
        m_copy(i).wait_send()
        x_copy(0, x, xr, i).wait_send()
        x_copy(1, g, gr, i).wait_send()
        o_copy(i).wait_send()
    for q in range(4):
        count = GROUP - (q == 0)
        group_wait(count, 0, sx, x3, y_send.at[0, q])
        group_wait(count, 0, sg, g3, y_send.at[1, q])
        group_wait(count, 0, b3, r3, b_send.at[q])
        d_copy(0, jnp.int32(q)).wait_send()
        d_copy(1, jnp.int32(q)).wait_send()
    for n in range(WIDE // TILE):
        for i in range(3):
            g_copy(i, n).wait()


def on_device(activations, out_grad, expert_ids, gate_probs, gate_weight, up_weight, down_weight):
    vmem = pl.BlockSpec(memory_space=pltpu.VMEM)
    hbm = pl.BlockSpec(memory_space=pl.ANY)
    dma = pltpu.SemaphoreType.DMA
    slabs = (4 * GROUP, SLAB, WIDE)
    grad = jax.ShapeDtypeStruct((1, WIDE, HID), BF)
    return tuple(
        pl.pallas_call(
            kernel,
            out_shape=(
                jax.ShapeDtypeStruct((TOK, 2 * WIDE), BF),
                jax.ShapeDtypeStruct((TOK, 1), BF),
                grad, grad, grad,
            ),
            in_specs=[vmem] * 4 + [hbm] * 5,
            out_specs=(vmem, vmem, hbm, hbm, hbm),
            scratch_shapes=[
                pltpu.VMEM((3, WIDE, HID), BF),
                pltpu.VMEM((4, 8, TOK), F32),
                pltpu.VMEM((4 * TOK, WIDE), BF),
                pltpu.VMEM((4 * TOK, WIDE), BF),
                pltpu.VMEM((4 * ROWS, 4 * TOK), BF),
                pltpu.VMEM((4 * ROWS, 4 * TOK), BF),
                pltpu.VMEM((4 * TOK, 4 * ROWS), BF),
                pltpu.VMEM(slabs, BF), pltpu.VMEM(slabs, BF),
                pltpu.VMEM(slabs, BF), pltpu.VMEM(slabs, BF),
                pltpu.VMEM((4, ROWS, 2 * HID), BF), pltpu.VMEM((4, ROWS, HID), BF),
                pltpu.VMEM((4, ROWS, 2 * HID), BF), pltpu.VMEM((4, ROWS, HID), BF),
                pltpu.VMEM((4 * ROWS, 2 * HID), BF), pltpu.VMEM((4 * ROWS, HID), BF),
                pltpu.VMEM((4 * GROUP, SLAB, WIDE + EXTRA), BF),
                pltpu.VMEM((4 * GROUP, SLAB, WIDE + EXTRA), BF),
                pltpu.VMEM((4, TOK, WIDE + EXTRA), BF),
                pltpu.VMEM((4, TOK, WIDE + EXTRA), BF),
                dma((3,)), dma((4,)), dma((4,)), dma((2, 4)), dma((2, 4)), dma((2, 4)), dma((2, 4)),
                dma((2, 4)), dma((2, 4)), dma((4,)), dma((4,)), dma((4,)), dma((4,)),
                dma((3, WIDE // TILE)),
            ],
            compiler_params=pltpu.CompilerParams(
                has_side_effects=True, vmem_limit_bytes=61 << 20
            ),
            cost_estimate=pl.CostEstimate(
                flops=8 * 2 * 4 * ROWS * WIDE * HID, bytes_accessed=6 * 2 * WIDE * HID, transcendentals=4 * ROWS * HID
            ),
        )(
            expert_ids,
            expert_ids.reshape(1, TOK),
            gate_probs.astype(F32).reshape(1, TOK),
            gate_probs,
            activations, out_grad, gate_weight, up_weight, down_weight,
        )
    )


def solution(mesh):
    rows, weights = P(("expert", "dp"), None), P("expert", "dp", None)
    return jax.shard_map(
        on_device,
        mesh=mesh,
        in_specs=(rows, rows, rows, rows, weights, weights, weights),
        out_specs=(rows, rows, weights, weights, weights),
        check_vma=False,
    )
```

time: 553 us -> 242 us (0.44); the launches traced: 542 us -> 241 us
  Pallas kernels: 0 us -> 223 us
  waiting for transfers between devices: 202 us -> 0 us
  blocking collectives: 128 us -> 0 us
  matrix products: 60.3 us -> 0 us
  local copies, waits for them, and re-layouts: 75.1 us -> 15.9 us
  starting transfers between devices: 46.3 us -> 0 us
  between operations: 14.9 us -> 0.64 us
  other arithmetic: 15.3 us -> 1.17 us
    pallas_call x0 -> x1, Pallas kernels: none -> 223 us  [on_device(): pl.pallas_call(kernel, out_shape=(jax.ShapeDtypeStruct((TOK, 2 * WIDE), B...]
    all_gather x3 -> x0, waiting for transfers between devices: 88.3 us -> none  [the longest x1 33.7 us: on_device(): hidden_rows = lax.all_gather(own_hidden, 'dp', axis=0, tiled=True)]
    all_to_all x7 -> x0, waiting for transfers between devices: 80.9 us -> none  [the longest x1 36.3 us: on_device(): lax.all_to_all(send_grads.reshape(expert_count, capacity, feature_width),...]
    all_to_all x2 -> x0, blocking collectives: 80.2 us -> none  [the longest x1 59.4 us: on_device(): lax.all_to_all(send_tokens.reshape(expert_count, capacity, feature_width)...]
    dot_general x9 -> x0, matrix products: 60.3 us -> none  [the longest x1 8.73 us: on_device(): jnp.einsum('rf,df->rd', accumulate_gate_rows, w_gate, preferred_element_t...]
    all_to_all x7 -> x0, starting transfers between devices: 45.4 us -> none  [the longest x1 10.8 us: on_device(): lax.all_to_all(returned_rows.reshape(expert_count, capacity, feature_widt...]
    all_gather x1 -> x0, blocking collectives: 41.5 us -> none  [on_device(): prob_rows = lax.all_gather(own_probs, 'dp', axis=0, tiled=True)]
    reduce_scatter x1 -> x0, waiting for transfers between devices: 31.7 us -> none  [on_device(): lax.psum_scatter(jnp.concatenate([jnp.dot(row_tokens, w_gate, preferred_e...]
  transfers between devices with their start and end apart: 11 -> 0, of which waited for: 8 -> 0; matrix products, arithmetic and copies ran while one was open for 15% -> 0% of each run, Pallas kernels for 0% -> 0%
where the time goes in v1:
time: 242 us; the launch traced here: 241 us
  Pallas kernels  223 us (92%)
  local copies, waits for them, and re-layouts  15.9 us (7%)
    pallas_call x1, Pallas kernels, on_device(): pl.pallas_call(kernel, out_shape=(jax.ShapeDtypeStruct((TOK, 2 * WIDE), B...  223 us
    unnamed x10, local copies, waits for them, and re-layouts  14.5 us

profile of v1, /device:TPU:0, one launch (start us, length us, event | category | flops | bytes accessed | tf_op | source)
XLA Modules:
  0.0 240.6 jit_solution(13811509812665721489)
XLA Ops:
  0.6 1.2 bitcast_convert_fusion.p_row
  1.8 1.4 copy.13.p_col
  3.2 1.4 copy.12.ids_col
  4.6 222.9 %shard_map.110 = (bf16[128,3584]{1,0:T(8,128)(2,1)}, bf16[128,1]{1,0:T(8,128)(2,1)}, bf16[1,1792,1024]{2,1,0:T(8,128)(2,1)}, bf16[1,1792,1024]{2,1,0:T(8,128)(2,1)}, bf16[1,1792,1024]{2,1,0:T(8,128)(2,1)}) custom-call(s32[128,1]{1,0:T(8,128)} %copy.12.ids_col, s32[1,128]{1,0:T(1,128)} %bitcast.4, f32[1,128]{1,0:T(1,128)} %bitcast_convert_fusion.p_row, ...), custom_call_target="tpu_custom_call" | custom-call | flops 22548578304 | bytes 22020096 | tf_op jit(solution)/shard_map/pallas_call | solution.py:328
  227.5 1.4 copy.14
  228.8 2.2 copy.19
  231.0 0.0 copy-start.1
  231.0 4.4 %copy.20 = bf16[1,1792,1024]{2,1,0:T(8,128)(2,1)} copy(bf16[1,1792,1024]{2,1,0:T(8,128)(2,1)} %get-tuple-element.17) | data formatting | bytes 7340032
  235.4 0.0 copy-done.1
  235.4 0.0 copy-start
  235.4 1.9 copy.21
  237.3 1.5 copy-done
  238.8 1.8 copy.22
Async XLA Ops:
  231.0 4.4 %copy-start.1 = (bf16[1,1792,1024]{2,1,0:T(8,128)(2,1)S(1)}, bf16[1,1792,1024]{2,1,0:T(8,128)(2,1)}, u32[]{:S(2)}) copy-start(bf16[1,1792,1024]{2,1,0:T(8,128)(2,1)} %get-tuple-element.18) | copy-start | bytes 11010052
  235.4 3.4 %copy-start = (bf16[1,1792,1024]{2,1,0:T(8,128)(2,1)S(1)}, bf16[1,1792,1024]{2,1,0:T(8,128)(2,1)}, u32[]{:S(2)}) copy-start(bf16[1,1792,1024]{2,1,0:T(8,128)(2,1)} %get-tuple-element.19) | copy-start | bytes 11010052

commit v2 on v1

v2 whole, which is shorter than its diff:
```python
import functools

import jax
import jax.numpy as jnp
from jax import lax
from jax.experimental import pallas as pl
from jax.experimental.pallas import tpu as pltpu
from jax.sharding import PartitionSpec as P

MESH = pl.DeviceIdType.MESH
BF = jnp.bfloat16
F32 = jnp.float32
TOK = 128
CAP = 6
SLAB = 4 * CAP
GROUP = 8
ROWS = GROUP * SLAB
WIDE = 1792
HID = 1024
EXTRA = 128
TILE = 256
CUT = 640


def rem(a, b):
    return lax.rem(a, jnp.int32(b))


def div(a, b):
    return lax.div(a, jnp.int32(b))


def dot(a, b, dims):
    return lax.dot_general(a, b, ((dims[:1], dims[1:]), ((), ())), preferred_element_type=F32)


def kernel(
    ids_row, p_row, x, g, wg, wu, wd,
    dx, dprob, vg, vu, vd,
    meta, xv, gv, px, pg, xr, gr, one, onep, onet, sx, sg, x3, g3,
    pgu, pr, qgu, qr, rows_gu, rows_h, b3, r3, out_s, out_r,
    w_sem, m_send, m_recv, x_send, x_recv, y_send, y_recv, d_send, d_recv,
    b_send, b_recv, o_send, o_recv,
):
    e = lax.axis_index("expert")
    xl = lax.axis_index("dp")
    core, xh, y, z = rem(e, 2), rem(div(e, 2), 2), rem(div(e, 4), 4), div(e, 16)
    mine = xh * 2 + xl
    own_slab = div(e, 4) * 2 + core

    def mate(i):
        th, tl = rem(xh + i // 2, 2), rem(xl + i % 2, 2)
        return th, tl, th * 2 + tl, (div(e, 4) * 4 + th * 2 + core, tl)

    def plane(q, sign):
        dz = rem(div(q * (q + 1), 2), 4)
        return rem(z + dz if sign > 0 else z + 4 - dz, 4)

    def half(ref, k):
        return ref.at[:, pl.ds(pl.multiple_of(k * WIDE, WIDE), WIDE)]

    def part(ref, m):
        return ref.at[pl.ds(pl.multiple_of(m * TOK, TOK), TOK)]

    def x_copy(a, i, src, dst, m, where):
        return pltpu.make_async_remote_copy(
            src_ref=src, dst_ref=part(dst, m),
            send_sem=x_send.at[a, i], recv_sem=x_recv.at[a, i],
            device_id=where, device_id_type=MESH,
        )

    def x_near(a, src, dst):
        return x_copy(a, 1, src, dst, mine, mate(1)[3])

    def x_over(a, src, dst):
        return x_copy(a, 3, half(src, 1 - xl), dst, mine, mate(3)[3])

    def x_pass(a, dst):
        m = mate(1)[2]
        return x_copy(a, 2, part(dst, m), dst, m, mate(3)[3])

    def x_own(a, src, dst):
        return pltpu.make_async_copy(half(src, xl), part(dst, mine), x_recv.at[a, 0])

    barrier = pltpu.get_barrier_semaphore()
    for i in (1, 2, 3):
        pl.semaphore_signal(barrier, inc=1, device_id=mate(i)[3], device_id_type=MESH)

    def greet(i, _):
        zt, yt = rem(z + div(i, GROUP), 4), rem(y + div(rem(i, GROUP), 2), 4)
        ct = rem(core + rem(i, 2), 2)
        pl.semaphore_signal(
            barrier, inc=1, device_id=(((zt * 4 + yt) * 2 + xh) * 2 + ct, xl), device_id_type=MESH
        )
        return 0

    lax.fori_loop(1, 4 * GROUP, greet, 0)

    load_x = pltpu.make_async_copy(x, xv, x_send.at[0, 0])
    load_g = pltpu.make_async_copy(g, gv, x_send.at[1, 0])
    load_x.start()
    load_g.start()
    x_own(0, x, xr).start()
    x_own(1, g, gr).start()
    for i, (w, v) in enumerate(((wg, vg), (wu, vu), (wd, vd))):
        pltpu.make_async_copy(w, v, w_sem.at[i]).start()

    ids = ids_row[...]
    side = ((ids >> 1) & 1).astype(F32)
    my_side = xh.astype(F32)
    stay = jnp.transpose(jnp.broadcast_to(side, (TOK, TOK))) == my_side

    def pack(src, dst):
        @pl.loop(0, WIDE // TOK)
        def _(n):
            far = src[:, pl.ds(pl.multiple_of((1 - xl) * WIDE + n * TOK, TOK), TOK)]
            near = src[:, pl.ds(pl.multiple_of(xl * WIDE + n * TOK, TOK), TOK)]
            dst[:, pl.ds(pl.multiple_of(n * TOK, TOK), TOK)] = jnp.where(
                stay, far.astype(F32), near.astype(F32)
            ).astype(BF)

    load_x.wait()
    pack(xv, px)
    pl.semaphore_wait(barrier, 4 * GROUP + 2)
    x_near(0, px, xr).start()
    x_over(0, x, xr).start()

    before = lax.broadcasted_iota(jnp.int32, (TOK, TOK), 0) < lax.broadcasted_iota(
        jnp.int32, (TOK, TOK), 1
    )
    wide_ids = jnp.broadcast_to(ids, (TOK, TOK)).astype(F32)
    same = jnp.where((jnp.transpose(wide_ids) == wide_ids) & before, 1.0, 0.0)
    rank = jnp.sum(same, axis=0, keepdims=True)
    row = ((ids >> 2) * 2 + (ids & 1)) * SLAB + mine * CAP
    meta[mine, 0:1, :] = side
    meta[mine, 1:2, :] = row.astype(F32) + rank
    meta[mine, 2:3, :] = p_row[...].astype(F32)
    meta[mine, 3:8, :] = jnp.zeros((5, TOK), F32)

    def m_copy(i):
        return pltpu.make_async_remote_copy(
            src_ref=meta.at[mine], dst_ref=meta.at[mine],
            send_sem=m_send.at[i], recv_sem=m_recv.at[i],
            device_id=mate(i)[3], device_id_type=MESH,
        )

    for i in (2, 1, 3):
        m_copy(i).start()
    load_g.wait()
    pack(gv, pg)
    x_near(1, pg, gr).start()

    x_near(0, px, xr).wait_recv()
    x_pass(0, xr).start()
    x_over(1, g, gr).start()

    for i in (1, 2, 3):
        m_copy(i).wait_recv()
    for m in range(4):
        want = jnp.where(meta[m, 0:1, :] == my_side, meta[m, 1:2, :], -1.0)
        prob = meta[m, 2:3, :]
        for r in range(4):
            at = lax.broadcasted_iota(jnp.int32, (ROWS, TOK), 0).astype(F32) + float(r * ROWS)
            hit = at == want
            one[r * ROWS : (r + 1) * ROWS, m * TOK : (m + 1) * TOK] = jnp.where(
                hit, 1.0, 0.0
            ).astype(BF)
            onep[r * ROWS : (r + 1) * ROWS, m * TOK : (m + 1) * TOK] = jnp.where(
                hit, prob, 0.0
            ).astype(BF)
        down = jnp.transpose(jnp.broadcast_to(want, (TOK, TOK)))
        for r in range(4 * ROWS // TOK):
            at = lax.broadcasted_iota(jnp.int32, (TOK, TOK), 1).astype(F32) + float(r * TOK)
            onet[m * TOK : (m + 1) * TOK, r * TOK : (r + 1) * TOK] = jnp.where(
                at == down, 1.0, 0.0
            ).astype(BF)

    def group_send(q, sign, src, dst, s_sem, r_sem, lanes=None):
        zt = plane(q, sign)

        def slab(ref, at):
            return ref.at[at] if lanes is None else ref.at[at, :, lanes]

        def one_send(i, _):
            yt, ct = rem(y + div(i, 2), 4), rem(core + rem(i, 2), 2)
            pltpu.make_async_remote_copy(
                src_ref=slab(src, (zt * 4 + yt) * 2 + ct), dst_ref=slab(dst, own_slab),
                send_sem=s_sem, recv_sem=r_sem,
                device_id=(((zt * 4 + yt) * 2 + xh) * 2 + ct, xl), device_id_type=MESH,
            ).start()
            return 0

        first = jnp.where(q == 0, 1, 0).astype(jnp.int32) if not isinstance(q, int) else int(q == 0)
        lax.fori_loop(first, GROUP, one_send, 0)

    def group_wait(count, first, src, dst, sem, lanes=slice(None)):
        pltpu.make_async_copy(
            src.at[pl.ds(first, count), :, lanes], dst.at[pl.ds(first, count), :, lanes], sem
        ).wait()

    def gather_and_send(a, order, picks, rows, src, dst):
        for q in order:
            zt = plane(jnp.int32(q), 1)

            @pl.loop(0, WIDE // TILE)
            def _(n):
                lanes = pl.ds(pl.multiple_of(n * TILE, TILE), TILE)
                here = pl.ds(pl.multiple_of(zt * ROWS, ROWS), ROWS)
                got = dot(picks[here, :], rows[:, lanes], (1, 0)).astype(BF)
                src[pl.ds(zt * GROUP, GROUP), :, lanes] = got.reshape(GROUP, SLAB, TILE)

            group_send(q, 1, src, dst, y_send.at[a, q], y_recv.at[a, q])
            if q == 0:
                pltpu.make_async_copy(src.at[own_slab], dst.at[own_slab], y_recv.at[a, 0]).start()

    x_near(1, pg, gr).wait_recv()
    x_pass(1, gr).start()
    x_over(0, x, xr).wait_recv()
    x_pass(0, xr).wait_recv()
    x_own(0, x, xr).wait()
    gather_and_send(0, (0, 1, 2, 3), one, xr, sx, x3)

    other = (e, 1 - xl)

    def d_copy(a, q):
        src, dst = ((pgu, qgu), (pr, qr))[a]
        at = plane(q, -1)
        return pltpu.make_async_remote_copy(
            src_ref=src.at[at], dst_ref=dst.at[at],
            send_sem=d_send.at[a, q], recv_sem=d_recv.at[a, q],
            device_id=other, device_id_type=MESH,
        )

    for i, (w, v) in enumerate(((wg, vg), (wu, vu), (wd, vd))):
        pltpu.make_async_copy(w, v, w_sem.at[i]).wait()

    def gate_and_up(q, _):
        at = plane(q, -1)
        group_wait(GROUP, at * GROUP, sx, x3, y_recv.at[0, q])

        @pl.loop(0, HID // TILE)
        def _(n):
            lanes = pl.ds(pl.multiple_of(n * TILE, TILE), TILE)
            more = pl.ds(pl.multiple_of(HID + n * TILE, TILE), TILE)
            left = x3[pl.ds(at * GROUP, GROUP)].reshape(ROWS, WIDE)
            pgu[at, :, lanes] = dot(left, vg[0, :, lanes], (1, 0)).astype(BF)
            pgu[at, :, more] = dot(left, vu[0, :, lanes], (1, 0)).astype(BF)

        d_copy(0, q).start()
        return 0

    lax.fori_loop(0, 1, gate_and_up, 0)
    x_over(1, g, gr).wait_recv()
    x_pass(1, gr).wait_recv()
    x_own(1, g, gr).wait()
    gather_and_send(1, (3, 2, 1, 0), onep, gr, sg, g3)

    lax.fori_loop(1, 4, gate_and_up, 0)

    @pl.loop(0, 4)
    def _(step):
        q = 3 - step
        at = plane(q, -1)
        group_wait(GROUP, at * GROUP, sg, g3, y_recv.at[1, q])

        @pl.loop(0, HID // TILE)
        def _(n):
            lanes = pl.ds(pl.multiple_of(n * TILE, TILE), TILE)
            left = g3[pl.ds(at * GROUP, GROUP)].reshape(ROWS, WIDE)
            pr[at, :, lanes] = dot(left, vd[0, :, lanes], (1, 0)).astype(BF)

        d_copy(1, q).start()

    for q in (3, 2, 1, 0):
        at = plane(jnp.int32(q), -1)
        d_copy(0, jnp.int32(q)).wait_recv()
        d_copy(1, jnp.int32(q)).wait_recv()
        here = pl.ds(pl.multiple_of(at * ROWS, ROWS), ROWS)

        def act(n, total):
            lanes = pl.ds(pl.multiple_of(n * TILE, TILE), TILE)
            more = pl.ds(pl.multiple_of(HID + n * TILE, TILE), TILE)
            gate = pgu[at, :, lanes].astype(F32) + qgu[at, :, lanes].astype(F32)
            up = pgu[at, :, more].astype(F32) + qgu[at, :, more].astype(F32)
            d = pr[at, :, lanes].astype(F32) + qr[at, :, lanes].astype(F32)
            s = jax.nn.sigmoid(gate)
            silu = gate * s
            hidden = silu * up
            rows_h[here, lanes] = hidden.astype(BF)
            rows_gu[here, lanes] = (d * up * (s * (1.0 + gate * (1.0 - s)))).astype(BF)
            rows_gu[here, more] = (d * silu).astype(BF)
            return total + jnp.sum(hidden * d, axis=1, keepdims=True)

        total = lax.fori_loop(0, HID // TILE, act, jnp.zeros((ROWS, 1), F32))
        b3[pl.ds(at * GROUP, GROUP), :, WIDE:] = (
            jnp.broadcast_to(total, (ROWS, EXTRA)).astype(BF).reshape(GROUP, SLAB, EXTRA)
        )

        def back(lanes):
            return dot(rows_gu[here, :HID], vg[0, lanes, :], (1, 1)) + dot(
                rows_gu[here, HID:], vu[0, lanes, :], (1, 1)
            )

        if q:

            @pl.loop(0, WIDE // TILE)
            def _(n):
                lanes = pl.ds(pl.multiple_of(n * TILE, TILE), TILE)
                slabs = back(lanes).astype(BF).reshape(GROUP, SLAB, TILE)
                b3[pl.ds(at * GROUP, GROUP), :, lanes] = slabs

            group_send(q, -1, b3, r3, b_send.at[q], b_recv.at[q])
        else:
            for c in range(3):
                width = min(CUT, WIDE - c * CUT)
                lanes = pl.ds(c * CUT, width)
                slabs = back(lanes).astype(BF).reshape(GROUP, SLAB, width)
                b3[pl.ds(at * GROUP, GROUP), :, lanes] = slabs
                sems, lanes = (b_send.at[4 + c], b_recv.at[4 + c]), pl.ds(c * CUT, CUT)
                group_send(q, -1, b3, r3, *sems, lanes)
                pltpu.make_async_copy(
                    b3.at[own_slab, :, lanes], r3.at[own_slab, :, lanes], sems[1]
                ).start()

    for q in (3, 2, 1):
        group_wait(GROUP, plane(jnp.int32(q), 1) * GROUP, b3, r3, b_recv.at[q])

    def o_copy(i, c):
        _, _, m, where = mate(i)
        lanes = pl.ds(c * CUT, CUT)
        return pltpu.make_async_remote_copy(
            src_ref=out_s.at[m, :, lanes], dst_ref=out_r.at[mine, :, lanes],
            send_sem=o_send.at[i, c], recv_sem=o_recv.at[i, c],
            device_id=where, device_id_type=MESH,
        )

    for c in range(3):
        lanes = pl.ds(c * CUT, CUT)
        group_wait(GROUP, z * GROUP, b3, r3, b_recv.at[4 + c], lanes)
        for i in (2, 1, 3, 0):
            m = mate(i)[2]
            picks = onet[pl.ds(pl.multiple_of(m * TOK, TOK), TOK), :]
            got = dot(picks, r3[:, :, lanes].reshape(4 * ROWS, CUT), (1, 0)).astype(BF)
            if i:
                out_s[m, :, lanes] = got
                o_copy(i, c).start()
            else:
                out_r[mine, :, lanes] = got

    @pl.loop(0, WIDE // TILE)
    def _(n):
        lanes = pl.ds(pl.multiple_of(n * TILE, TILE), TILE)
        left = g3[:, :, lanes].reshape(4 * ROWS, TILE)
        vd[0, lanes, :] = dot(left, rows_h[...], (0, 0)).astype(BF)
        left = x3[:, :, lanes].reshape(4 * ROWS, TILE)
        vg[0, lanes, :] = dot(left, rows_gu[:, :HID], (0, 0)).astype(BF)
        vu[0, lanes, :] = dot(left, rows_gu[:, HID:], (0, 0)).astype(BF)

    for c in range(3):
        for i in (1, 2, 3):
            o_copy(i, c).wait_recv()
    for k in range(2):
        dx[:, k * WIDE : (k + 1) * WIDE] = (
            out_r[k, :, :WIDE].astype(F32) + out_r[2 + k, :, :WIDE].astype(F32)
        ).astype(BF)
    term = jnp.transpose(out_r[0, :, WIDE:].astype(F32) + out_r[2, :, WIDE:].astype(F32))
    dprob[...] = (term[0:1] / p_row[...].astype(F32)).astype(BF)

    for i in (1, 2, 3):
        m_copy(i).wait_send()
        for c in range(3):
            o_copy(i, c).wait_send()
    for c in range(3):
        group_wait(GROUP - 1, 0, b3, r3, b_send.at[4 + c], pl.ds(c * CUT, CUT))
    for a, (src, packed, dst) in enumerate(((x, px, xr), (g, pg, gr))):
        x_near(a, packed, dst).wait_send()
        x_over(a, src, dst).wait_send()
        x_pass(a, dst).wait_send()
    for q in range(4):
        count = GROUP - (q == 0)
        group_wait(count, 0, sx, x3, y_send.at[0, q])
        group_wait(count, 0, sg, g3, y_send.at[1, q])
        if q:
            group_wait(count, 0, b3, r3, b_send.at[q])
        d_copy(0, jnp.int32(q)).wait_send()
        d_copy(1, jnp.int32(q)).wait_send()


def place(*refs):
    count = (len(refs) - 1) // 2
    copies = [
        pltpu.make_async_copy(refs[i], refs[count + i], refs[-1].at[i]) for i in range(count)
    ]
    for copy in copies:
        copy.start()
    for copy in copies:
        copy.wait()


def on_device(activations, out_grad, expert_ids, gate_probs, gate_weight, up_weight, down_weight):
    vmem = pl.BlockSpec(memory_space=pltpu.VMEM)
    hbm = pl.BlockSpec(memory_space=pl.ANY)
    dma = pltpu.SemaphoreType.DMA
    slabs = (4 * GROUP, SLAB, WIDE)
    grad = pltpu.VMEM((1, WIDE, HID), BF)
    dx, dprob, *grads = (
        pl.pallas_call(
            kernel,
            out_shape=(
                pltpu.VMEM((TOK, 2 * WIDE), BF),
                pltpu.VMEM((1, TOK), BF),
                grad, grad, grad,
            ),
            in_specs=[vmem] * 2 + [hbm] * 5,
            out_specs=(vmem,) * 5,
            scratch_shapes=[
                pltpu.VMEM((4, 8, TOK), F32),
                pltpu.VMEM((TOK, 2 * WIDE), BF), pltpu.VMEM((TOK, 2 * WIDE), BF),
                pltpu.VMEM((TOK, WIDE), BF), pltpu.VMEM((TOK, WIDE), BF),
                pltpu.VMEM((4 * TOK, WIDE), BF),
                pltpu.VMEM((4 * TOK, WIDE), BF),
                pltpu.VMEM((4 * ROWS, 4 * TOK), BF),
                pltpu.VMEM((4 * ROWS, 4 * TOK), BF),
                pltpu.VMEM((4 * TOK, 4 * ROWS), BF),
                pltpu.VMEM(slabs, BF), pltpu.VMEM(slabs, BF),
                pltpu.VMEM(slabs, BF), pltpu.VMEM(slabs, BF),
                pltpu.VMEM((4, ROWS, 2 * HID), BF), pltpu.VMEM((4, ROWS, HID), BF),
                pltpu.VMEM((4, ROWS, 2 * HID), BF), pltpu.VMEM((4, ROWS, HID), BF),
                pltpu.VMEM((4 * ROWS, 2 * HID), BF), pltpu.VMEM((4 * ROWS, HID), BF),
                pltpu.VMEM((4 * GROUP, SLAB, WIDE + EXTRA), BF),
                pltpu.VMEM((4 * GROUP, SLAB, WIDE + EXTRA), BF),
                pltpu.VMEM((4, TOK, WIDE + EXTRA), BF),
                pltpu.VMEM((4, TOK, WIDE + EXTRA), BF),
                dma((3,)), dma((4,)), dma((4,)), dma((2, 4)), dma((2, 4)), dma((2, 4)), dma((2, 4)),
                dma((2, 4)), dma((2, 4)), dma((7,)), dma((7,)), dma((4, 3)), dma((4, 3)),
            ],
            compiler_params=pltpu.CompilerParams(
                has_side_effects=True, collective_id=0, vmem_limit_bytes=49 << 20
            ),
            cost_estimate=pl.CostEstimate(
                flops=8 * 2 * 4 * ROWS * WIDE * HID, bytes_accessed=6 * 2 * WIDE * HID, transcendentals=4 * ROWS * HID
            ),
        )(
            expert_ids.reshape(1, TOK),
            gate_probs.reshape(1, TOK),
            activations, out_grad, gate_weight, up_weight, down_weight,
        )
    )
    made = [pltpu.with_memory_space_constraint(a, pltpu.VMEM) for a in (dx, dprob, *grads)]
    dx, dprob, *grads = pl.pallas_call(
        place,
        out_shape=[jax.ShapeDtypeStruct(a.shape, a.dtype) for a in made],
        in_specs=[vmem] * 5,
        out_specs=[hbm] * 5,
        scratch_shapes=[dma((5,))],
        compiler_params=pltpu.CompilerParams(vmem_limit_bytes=1 << 20),
    )(*made)
    return dx, dprob.reshape(TOK, 1), *grads


def solution(mesh):
    rows, weights = P(("expert", "dp"), None), P("expert", "dp", None)
    return jax.shard_map(
        on_device,
        mesh=mesh,
        in_specs=(rows, rows, rows, rows, weights, weights, weights),
        out_specs=(rows, rows, weights, weights, weights),
        check_vma=False,
    )
```

time: 242 us -> 200 us (0.83)
  Pallas kernels: 223 us -> 199 us
  local copies, waits for them, and re-layouts: 15.9 us -> 0 us
    pallas_call x1 -> x2, Pallas kernels: 223 us -> 199 us  [the longest x1 195 us: on_device(): pl.pallas_call(kernel, out_shape=(pltpu.VMEM((TOK, 2 * WIDE), BF), pltpu....]
    unnamed x10 -> x0, local copies, waits for them, and re-layouts: 14.5 us -> none
where the time goes in v2:
time: 200 us
  Pallas kernels  199 us (100%)
    pallas_call x1, Pallas kernels, on_device(): pl.pallas_call(kernel, out_shape=(pltpu.VMEM((TOK, 2 * WIDE), BF), pltpu....  195 us
    pallas_call x1, Pallas kernels, on_device(): pl.pallas_call(place, out_shape=[jax.ShapeDtypeStruct(a.shape, a.dtype) f...  4.5 us

profile of v2, /device:TPU:0, one launch (start us, length us, event | category | flops | bytes accessed | tf_op | source)
XLA Modules:
  0.0 200.0 jit_solution(3576358626835610340)
XLA Ops:
  0.6 194.9 %shard_map.110 = (bf16[128,3584]{1,0:T(8,128)(2,1)S(1)}, bf16[1,128]{1,0:T(2,128)(2,1)S(1)}, bf16[1,1792,1024]{2,1,0:T(8,128)(2,1)S(1)}, bf16[1,1792,1024]{2,1,0:T(8,128)(2,1)S(1)}, bf16[1,1792,1024]{2,1,0:T(8,128)(2,1)S(1)}) custom-call(s32[1,128]{1,0:T(1,128)} %bitcast.3, bf16[1,128]{1,0:T(2,128)(2,1)} %bitcast.4, bf16[128,3584]{1,0:T(8,128)(2,1)} %x.1, ...), custom_call_target="tpu_custom_call" | custom-call | flops 22548578304 | bytes 22020096 | tf_op jit(solution)/shard_map/pallas_call | solution.py:407
  195.5 4.5 %shard_map.111 = (bf16[128,3584]{1,0:T(8,128)(2,1)}, bf16[1,128]{1,0:T(2,128)(2,1)}, bf16[1,1792,1024]{2,1,0:T(8,128)(2,1)}, bf16[1,1792,1024]{2,1,0:T(8,128)(2,1)}, bf16[1,1792,1024]{2,1,0:T(8,128)(2,1)}) custom-call(bf16[128,3584]{1,0:T(8,128)(2,1)S(1)} %get-tuple-element.15.refs_0_, bf16[1,128]{1,0:T(2,128)(2,1)S(1)} %get-tuple-element.16.refs_1_, ...), custom_call_target="tpu_custom_call" | custom-call | tf_op jit(solution)/shard_map/pallas_call | solution.py:450

commit v3 on v2

--- a/solution.py
+++ b/solution.py
@@ -19,7 +19,7 @@
 HID = 1024
 EXTRA = 128
 TILE = 256
-CUT = 640
+PIECES = ((0, 3), (3, 5), (5, 7))
 
 
 def rem(a, b):
@@ -190,7 +190,7 @@
             ).start()
             return 0
 
-        first = jnp.where(q == 0, 1, 0).astype(jnp.int32) if not isinstance(q, int) else int(q == 0)
+        first = jnp.where(q == 0, 1, 0).astype(jnp.int32)
         lax.fori_loop(first, GROUP, one_send, 0)
 
     def group_wait(count, first, src, dst, sem, lanes=slice(None)):
@@ -198,9 +198,11 @@
             src.at[pl.ds(first, count), :, lanes], dst.at[pl.ds(first, count), :, lanes], sem
         ).wait()
 
-    def gather_and_send(a, order, picks, rows, src, dst):
-        for q in order:
-            zt = plane(jnp.int32(q), 1)
+    def gather_and_send(a, turn, picks, rows, src, dst):
+        @pl.loop(0, 4)
+        def _(step):
+            q = turn(step)
+            zt = plane(q, 1)
 
             @pl.loop(0, WIDE // TILE)
             def _(n):
@@ -210,7 +212,9 @@
                 src[pl.ds(zt * GROUP, GROUP), :, lanes] = got.reshape(GROUP, SLAB, TILE)
 
             group_send(q, 1, src, dst, y_send.at[a, q], y_recv.at[a, q])
-            if q == 0:
+
+            @pl.when(q == 0)
+            def _():
                 pltpu.make_async_copy(src.at[own_slab], dst.at[own_slab], y_recv.at[a, 0]).start()
 
     x_near(1, pg, gr).wait_recv()
@@ -218,7 +222,7 @@
     x_over(0, x, xr).wait_recv()
     x_pass(0, xr).wait_recv()
     x_own(0, x, xr).wait()
-    gather_and_send(0, (0, 1, 2, 3), one, xr, sx, x3)
+    gather_and_send(0, lambda step: step, one, xr, sx, x3)
 
     other = (e, 1 - xl)
 
@@ -253,7 +257,7 @@
     x_over(1, g, gr).wait_recv()
     x_pass(1, gr).wait_recv()
     x_own(1, g, gr).wait()
-    gather_and_send(1, (3, 2, 1, 0), onep, gr, sg, g3)
+    gather_and_send(1, lambda step: 3 - step, onep, gr, sg, g3)
 
     lax.fori_loop(1, 4, gate_and_up, 0)
 
@@ -271,10 +275,16 @@
 
         d_copy(1, q).start()
 
-    for q in (3, 2, 1, 0):
-        at = plane(jnp.int32(q), -1)
-        d_copy(0, jnp.int32(q)).wait_recv()
-        d_copy(1, jnp.int32(q)).wait_recv()
+    def piece(c):
+        first, end = PIECES[c]
+        return pl.ds(first * TILE, (end - first) * TILE + (EXTRA if c == 2 else 0))
+
+    @pl.loop(0, 4)
+    def _(step):
+        q = 3 - step
+        at = plane(q, -1)
+        d_copy(0, q).wait_recv()
+        d_copy(1, q).wait_recv()
         here = pl.ds(pl.multiple_of(at * ROWS, ROWS), ROWS)
 
         def act(n, total):
@@ -296,56 +306,58 @@
             jnp.broadcast_to(total, (ROWS, EXTRA)).astype(BF).reshape(GROUP, SLAB, EXTRA)
         )
 
-        def back(lanes):
-            return dot(rows_gu[here, :HID], vg[0, lanes, :], (1, 1)) + dot(
+        @pl.loop(0, WIDE // TILE)
+        def _(n):
+            lanes = pl.ds(pl.multiple_of(n * TILE, TILE), TILE)
+            back = dot(rows_gu[here, :HID], vg[0, lanes, :], (1, 1)) + dot(
                 rows_gu[here, HID:], vu[0, lanes, :], (1, 1)
             )
-
-        if q:
-
-            @pl.loop(0, WIDE // TILE)
-            def _(n):
-                lanes = pl.ds(pl.multiple_of(n * TILE, TILE), TILE)
-                slabs = back(lanes).astype(BF).reshape(GROUP, SLAB, TILE)
-                b3[pl.ds(at * GROUP, GROUP), :, lanes] = slabs
-
-            group_send(q, -1, b3, r3, b_send.at[q], b_recv.at[q])
-        else:
+            b3[pl.ds(at * GROUP, GROUP), :, lanes] = back.astype(BF).reshape(GROUP, SLAB, TILE)
             for c in range(3):
-                width = min(CUT, WIDE - c * CUT)
-                lanes = pl.ds(c * CUT, width)
-                slabs = back(lanes).astype(BF).reshape(GROUP, SLAB, width)
-                b3[pl.ds(at * GROUP, GROUP), :, lanes] = slabs
-                sems, lanes = (b_send.at[4 + c], b_recv.at[4 + c]), pl.ds(c * CUT, CUT)
-                group_send(q, -1, b3, r3, *sems, lanes)
-                pltpu.make_async_copy(
-                    b3.at[own_slab, :, lanes], r3.at[own_slab, :, lanes], sems[1]
-                ).start()
-
-    for q in (3, 2, 1):
-        group_wait(GROUP, plane(jnp.int32(q), 1) * GROUP, b3, r3, b_recv.at[q])
+
+                @pl.when(n == PIECES[c][1] - 1)
+                def _(c=c):
+                    sems = b_send.at[q, c], b_recv.at[q, c]
+                    group_send(q, -1, b3, r3, *sems, piece(c))
+
+                    @pl.when(q == 0)
+                    def _():
+                        pltpu.make_async_copy(
+                            b3.at[own_slab, :, piece(c)], r3.at[own_slab, :, piece(c)], sems[1]
+                        ).start()
 
     def o_copy(i, c):
         _, _, m, where = mate(i)
-        lanes = pl.ds(c * CUT, CUT)
         return pltpu.make_async_remote_copy(
-            src_ref=out_s.at[m, :, lanes], dst_ref=out_r.at[mine, :, lanes],
+            src_ref=out_s.at[m, :, piece(c)], dst_ref=out_r.at[mine, :, piece(c)],
             send_sem=o_send.at[i, c], recv_sem=o_recv.at[i, c],
             device_id=where, device_id_type=MESH,
         )
 
-    for c in range(3):
-        lanes = pl.ds(c * CUT, CUT)
-        group_wait(GROUP, z * GROUP, b3, r3, b_recv.at[4 + c], lanes)
-        for i in (2, 1, 3, 0):
-            m = mate(i)[2]
-            picks = onet[pl.ds(pl.multiple_of(m * TOK, TOK), TOK), :]
-            got = dot(picks, r3[:, :, lanes].reshape(4 * ROWS, CUT), (1, 0)).astype(BF)
-            if i:
-                out_s[m, :, lanes] = got
-                o_copy(i, c).start()
-            else:
-                out_r[mine, :, lanes] = got
+    def pick(lanes, width):
+        got = dot(onet[...], r3[:, :, lanes].reshape(4 * ROWS, width), (1, 0))
+        out_s[:, :, lanes] = got.astype(BF).reshape(4, TOK, width)
+        out_r[mine, :, lanes] = out_s[mine, :, lanes]
+
+    @pl.loop(0, WIDE // TILE)
+    def _(n):
+        for c in range(3):
+
+            @pl.when(n == PIECES[c][0])
+            def _(c=c):
+                for q in (3, 2, 1, 0):
+                    at = plane(jnp.int32(q), 1)
+                    group_wait(GROUP, at * GROUP, b3, r3, b_recv.at[q, c], piece(c))
+
+        pick(pl.ds(pl.multiple_of(n * TILE, TILE), TILE), TILE)
+        for c in range(3):
+
+            @pl.when(n == PIECES[c][1] - 1)
+            def _(c=c):
+                if c == 2:
+                    pick(pl.ds(WIDE, EXTRA), EXTRA)
+                for i in (2, 1, 3):
+                    o_copy(i, c).start()
 
     @pl.loop(0, WIDE // TILE)
     def _(n):
@@ -370,8 +382,6 @@
         m_copy(i).wait_send()
         for c in range(3):
             o_copy(i, c).wait_send()
-    for c in range(3):
-        group_wait(GROUP - 1, 0, b3, r3, b_send.at[4 + c], pl.ds(c * CUT, CUT))
     for a, (src, packed, dst) in enumerate(((x, px, xr), (g, pg, gr))):
         x_near(a, packed, dst).wait_send()
         x_over(a, src, dst).wait_send()
@@ -380,8 +390,8 @@
         count = GROUP - (q == 0)
         group_wait(count, 0, sx, x3, y_send.at[0, q])
         group_wait(count, 0, sg, g3, y_send.at[1, q])
-        if q:
-            group_wait(count, 0, b3, r3, b_send.at[q])
+        for c in range(3):
+            group_wait(count, 0, b3, r3, b_send.at[q, c], piece(c))
         d_copy(0, jnp.int32(q)).wait_send()
         d_copy(1, jnp.int32(q)).wait_send()
 
@@ -432,7 +442,7 @@
                 pltpu.VMEM((4, TOK, WIDE + EXTRA), BF),
                 pltpu.VMEM((4, TOK, WIDE + EXTRA), BF),
                 dma((3,)), dma((4,)), dma((4,)), dma((2, 4)), dma((2, 4)), dma((2, 4)), dma((2, 4)),
-                dma((2, 4)), dma((2, 4)), dma((7,)), dma((7,)), dma((4, 3)), dma((4, 3)),
+                dma((2, 4)), dma((2, 4)), dma((4, 3)), dma((4, 3)), dma((4, 3)), dma((4, 3)),
             ],
             compiler_params=pltpu.CompilerParams(
                 has_side_effects=True, collective_id=0, vmem_limit_bytes=49 << 20

time: 200 us -> 197 us (0.985)
  Pallas kernels: 199 us -> 196 us
    pallas_call x1, Pallas kernels: 195 us -> 192 us  [on_device(): pl.pallas_call(kernel, out_shape=(pltpu.VMEM((TOK, 2 * WIDE), BF), pltpu....]
where the time goes in v3:
time: 197 us
  Pallas kernels  196 us (99%)
    pallas_call x1, Pallas kernels, on_device(): pl.pallas_call(kernel, out_shape=(pltpu.VMEM((TOK, 2 * WIDE), BF), pltpu....  192 us
    pallas_call x1, Pallas kernels, on_device(): pl.pallas_call(place, out_shape=[jax.ShapeDtypeStruct(a.shape, a.dtype) f...  4.5 us

profile of v3, /device:TPU:0, one launch (start us, length us, event | category | flops | bytes accessed | tf_op | source)
XLA Modules:
  0.0 196.7 jit_solution(13660274762991005159)
XLA Ops:
  0.6 191.6 %shard_map.110 = (bf16[128,3584]{1,0:T(8,128)(2,1)S(1)}, bf16[1,128]{1,0:T(2,128)(2,1)S(1)}, bf16[1,1792,1024]{2,1,0:T(8,128)(2,1)S(1)}, bf16[1,1792,1024]{2,1,0:T(8,128)(2,1)S(1)}, bf16[1,1792,1024]{2,1,0:T(8,128)(2,1)S(1)}) custom-call(s32[1,128]{1,0:T(1,128)} %bitcast.3, bf16[1,128]{1,0:T(2,128)(2,1)} %bitcast.4, bf16[128,3584]{1,0:T(8,128)(2,1)} %x.1, ...), custom_call_target="tpu_custom_call" | custom-call | flops 22548578304 | bytes 22020096 | tf_op jit(solution)/shard_map/pallas_call | solution.py:417
  192.2 4.5 %shard_map.111 = (bf16[128,3584]{1,0:T(8,128)(2,1)}, bf16[1,128]{1,0:T(2,128)(2,1)}, bf16[1,1792,1024]{2,1,0:T(8,128)(2,1)}, bf16[1,1792,1024]{2,1,0:T(8,128)(2,1)}, bf16[1,1792,1024]{2,1,0:T(8,128)(2,1)}) custom-call(bf16[128,3584]{1,0:T(8,128)(2,1)S(1)} %get-tuple-element.15.refs_0_, bf16[1,128]{1,0:T(2,128)(2,1)S(1)} %get-tuple-element.16.refs_1_, ...), custom_call_target="tpu_custom_call" | custom-call | tf_op jit(solution)/shard_map/pallas_call | solution.py:460

commit v4 on v3

--- a/solution.py
+++ b/solution.py
@@ -46,15 +46,18 @@
     xl = lax.axis_index("dp")
     core, xh, y, z = rem(e, 2), rem(div(e, 2), 2), rem(div(e, 4), 4), div(e, 16)
     mine = xh * 2 + xl
-    own_slab = div(e, 4) * 2 + core
 
     def mate(i):
         th, tl = rem(xh + i // 2, 2), rem(xl + i % 2, 2)
         return th, tl, th * 2 + tl, (div(e, 4) * 4 + th * 2 + core, tl)
 
-    def plane(q, sign):
-        dz = rem(div(q * (q + 1), 2), 4)
-        return rem(z + dz if sign > 0 else z + 4 - dz, 4)
+    def place_of(q, i, sign):
+        dz = div(i, 2)
+        dy = rem(dz + q, 4)
+        zt = rem(z + dz if sign > 0 else z + 4 - dz, 4)
+        yt = rem(y + dy if sign > 0 else y + 4 - dy, 4)
+        ct = rem(core + rem(i, 2), 2)
+        return (((zt * 4 + yt) * 2 + xh) * 2 + ct, xl)
 
     def half(ref, k):
         return ref.at[:, pl.ds(pl.multiple_of(k * WIDE, WIDE), WIDE)]
@@ -131,7 +134,10 @@
     wide_ids = jnp.broadcast_to(ids, (TOK, TOK)).astype(F32)
     same = jnp.where((jnp.transpose(wide_ids) == wide_ids) & before, 1.0, 0.0)
     rank = jnp.sum(same, axis=0, keepdims=True)
-    row = ((ids >> 2) * 2 + (ids & 1)) * SLAB + mine * CAP
+    dz = ((ids >> 4) + 4 - z) & 3
+    dy = (((ids >> 2) & 3) + 4 - y) & 3
+    slab = ((dy + 4 - dz) & 3) * GROUP + dz * 2 + (((ids & 1) + core) & 1)
+    row = slab * SLAB + mine * CAP
     meta[mine, 0:1, :] = side
     meta[mine, 1:2, :] = row.astype(F32) + rank
     meta[mine, 2:3, :] = p_row[...].astype(F32)
@@ -175,18 +181,13 @@
                 at == down, 1.0, 0.0
             ).astype(BF)
 
-    def group_send(q, sign, src, dst, s_sem, r_sem, lanes=None):
-        zt = plane(q, sign)
-
-        def slab(ref, at):
-            return ref.at[at] if lanes is None else ref.at[at, :, lanes]
-
+    def group_send(q, sign, src, dst, s_sem, r_sem, lanes=slice(None)):
         def one_send(i, _):
-            yt, ct = rem(y + div(i, 2), 4), rem(core + rem(i, 2), 2)
+            at = q * GROUP + i
             pltpu.make_async_remote_copy(
-                src_ref=slab(src, (zt * 4 + yt) * 2 + ct), dst_ref=slab(dst, own_slab),
+                src_ref=src.at[at, :, lanes], dst_ref=dst.at[at, :, lanes],
                 send_sem=s_sem, recv_sem=r_sem,
-                device_id=(((zt * 4 + yt) * 2 + xh) * 2 + ct, xl), device_id_type=MESH,
+                device_id=place_of(q, i, sign), device_id_type=MESH,
             ).start()
             return 0
 
@@ -202,20 +203,19 @@
         @pl.loop(0, 4)
         def _(step):
             q = turn(step)
-            zt = plane(q, 1)
 
             @pl.loop(0, WIDE // TILE)
             def _(n):
                 lanes = pl.ds(pl.multiple_of(n * TILE, TILE), TILE)
-                here = pl.ds(pl.multiple_of(zt * ROWS, ROWS), ROWS)
+                here = pl.ds(pl.multiple_of(q * ROWS, ROWS), ROWS)
                 got = dot(picks[here, :], rows[:, lanes], (1, 0)).astype(BF)
-                src[pl.ds(zt * GROUP, GROUP), :, lanes] = got.reshape(GROUP, SLAB, TILE)
+                src[pl.ds(q * GROUP, GROUP), :, lanes] = got.reshape(GROUP, SLAB, TILE)
 
             group_send(q, 1, src, dst, y_send.at[a, q], y_recv.at[a, q])
 
             @pl.when(q == 0)
             def _():
-                pltpu.make_async_copy(src.at[own_slab], dst.at[own_slab], y_recv.at[a, 0]).start()
+                pltpu.make_async_copy(src.at[0], dst.at[0], y_recv.at[a, 0]).start()
 
     x_near(1, pg, gr).wait_recv()
     x_pass(1, gr).start()
@@ -228,7 +228,7 @@
 
     def d_copy(a, q):
         src, dst = ((pgu, qgu), (pr, qr))[a]
-        at = plane(q, -1)
+        at = q
         return pltpu.make_async_remote_copy(
             src_ref=src.at[at], dst_ref=dst.at[at],
             send_sem=d_send.at[a, q], recv_sem=d_recv.at[a, q],
@@ -239,7 +239,7 @@
         pltpu.make_async_copy(w, v, w_sem.at[i]).wait()
 
     def gate_and_up(q, _):
-        at = plane(q, -1)
+        at = q
         group_wait(GROUP, at * GROUP, sx, x3, y_recv.at[0, q])
 
         @pl.loop(0, HID // TILE)
@@ -257,14 +257,14 @@
     x_over(1, g, gr).wait_recv()
     x_pass(1, gr).wait_recv()
     x_own(1, g, gr).wait()
-    gather_and_send(1, lambda step: 3 - step, onep, gr, sg, g3)
+    gather_and_send(1, lambda step: step, onep, gr, sg, g3)
 
     lax.fori_loop(1, 4, gate_and_up, 0)
 
     @pl.loop(0, 4)
     def _(step):
-        q = 3 - step
-        at = plane(q, -1)
+        q = step
+        at = q
         group_wait(GROUP, at * GROUP, sg, g3, y_recv.at[1, q])
 
         @pl.loop(0, HID // TILE)
@@ -281,8 +281,8 @@
 
     @pl.loop(0, 4)
     def _(step):
-        q = 3 - step
-        at = plane(q, -1)
+        q = step
+        at = q
         d_copy(0, q).wait_recv()
         d_copy(1, q).wait_recv()
         here = pl.ds(pl.multiple_of(at * ROWS, ROWS), ROWS)
@@ -323,7 +323,7 @@
                     @pl.when(q == 0)
                     def _():
                         pltpu.make_async_copy(
-                            b3.at[own_slab, :, piece(c)], r3.at[own_slab, :, piece(c)], sems[1]
+                            b3.at[0, :, piece(c)], r3.at[0, :, piece(c)], sems[1]
                         ).start()
 
     def o_copy(i, c):
@@ -346,8 +346,7 @@
             @pl.when(n == PIECES[c][0])
             def _(c=c):
                 for q in (3, 2, 1, 0):
-                    at = plane(jnp.int32(q), 1)
-                    group_wait(GROUP, at * GROUP, b3, r3, b_recv.at[q, c], piece(c))
+                    group_wait(GROUP, q * GROUP, b3, r3, b_recv.at[q, c], piece(c))
 
         pick(pl.ds(pl.multiple_of(n * TILE, TILE), TILE), TILE)
         for c in range(3):

time: 197 us -> 193 us (0.980)
  Pallas kernels: 196 us -> 192 us
    pallas_call x1, Pallas kernels: 192 us -> 188 us  [on_device(): pl.pallas_call(kernel, out_shape=(pltpu.VMEM((TOK, 2 * WIDE), BF), pltpu....]
where the time goes in v4:
time: 193 us
  Pallas kernels  192 us (99%)
    pallas_call x1, Pallas kernels, on_device(): pl.pallas_call(kernel, out_shape=(pltpu.VMEM((TOK, 2 * WIDE), BF), pltpu....  188 us
    pallas_call x1, Pallas kernels, on_device(): pl.pallas_call(place, out_shape=[jax.ShapeDtypeStruct(a.shape, a.dtype) f...  4.5 us

profile of v4, /device:TPU:0, one launch (start us, length us, event | category | flops | bytes accessed | tf_op | source)
XLA Modules:
  0.0 193.1 jit_solution(1979588958906577731)
XLA Ops:
  0.6 188.0 %shard_map.110 = (bf16[128,3584]{1,0:T(8,128)(2,1)S(1)}, bf16[1,128]{1,0:T(2,128)(2,1)S(1)}, bf16[1,1792,1024]{2,1,0:T(8,128)(2,1)S(1)}, bf16[1,1792,1024]{2,1,0:T(8,128)(2,1)S(1)}, bf16[1,1792,1024]{2,1,0:T(8,128)(2,1)S(1)}) custom-call(s32[1,128]{1,0:T(1,128)} %bitcast.3, bf16[1,128]{1,0:T(2,128)(2,1)} %bitcast.4, bf16[128,3584]{1,0:T(8,128)(2,1)} %x.1, ...), custom_call_target="tpu_custom_call" | custom-call | flops 22548578304 | bytes 22020096 | tf_op jit(solution)/shard_map/pallas_call | solution.py:416
  188.6 4.5 %shard_map.111 = (bf16[128,3584]{1,0:T(8,128)(2,1)}, bf16[1,128]{1,0:T(2,128)(2,1)}, bf16[1,1792,1024]{2,1,0:T(8,128)(2,1)}, bf16[1,1792,1024]{2,1,0:T(8,128)(2,1)}, bf16[1,1792,1024]{2,1,0:T(8,128)(2,1)}) custom-call(bf16[128,3584]{1,0:T(8,128)(2,1)S(1)} %get-tuple-element.15.refs_0_, bf16[1,128]{1,0:T(2,128)(2,1)S(1)} %get-tuple-element.16.refs_1_, ...), custom_call_target="tpu_custom_call" | custom-call | tf_op jit(solution)/shard_map/pallas_call | solution.py:459

commit v5 on v4

--- a/solution.py
+++ b/solution.py
@@ -19,7 +19,7 @@
 HID = 1024
 EXTRA = 128
 TILE = 256
-PIECES = ((0, 3), (3, 5), (5, 7))
+PIECES = ((0, 2), (2, 4), (4, 6), (6, 7))
 
 
 def rem(a, b):
@@ -182,7 +182,10 @@
             ).astype(BF)
 
     def group_send(q, sign, src, dst, s_sem, r_sem, lanes=slice(None)):
-        def one_send(i, _):
+        first = jnp.where(q == 0, 1, 0).astype(jnp.int32)
+
+        def one_send(step, _):
+            i = GROUP - 1 + first - step
             at = q * GROUP + i
             pltpu.make_async_remote_copy(
                 src_ref=src.at[at, :, lanes], dst_ref=dst.at[at, :, lanes],
@@ -191,7 +194,6 @@
             ).start()
             return 0
 
-        first = jnp.where(q == 0, 1, 0).astype(jnp.int32)
         lax.fori_loop(first, GROUP, one_send, 0)
 
     def group_wait(count, first, src, dst, sem, lanes=slice(None)):
@@ -277,7 +279,7 @@
 
     def piece(c):
         first, end = PIECES[c]
-        return pl.ds(first * TILE, (end - first) * TILE + (EXTRA if c == 2 else 0))
+        return pl.ds(first * TILE, (end - first) * TILE + (EXTRA if c == 3 else 0))
 
     @pl.loop(0, 4)
     def _(step):
@@ -313,7 +315,7 @@
                 rows_gu[here, HID:], vu[0, lanes, :], (1, 1)
             )
             b3[pl.ds(at * GROUP, GROUP), :, lanes] = back.astype(BF).reshape(GROUP, SLAB, TILE)
-            for c in range(3):
+            for c in range(4):
 
                 @pl.when(n == PIECES[c][1] - 1)
                 def _(c=c):
@@ -341,7 +343,7 @@
 
     @pl.loop(0, WIDE // TILE)
     def _(n):
-        for c in range(3):
+        for c in range(4):
 
             @pl.when(n == PIECES[c][0])
             def _(c=c):
@@ -349,11 +351,11 @@
                     group_wait(GROUP, q * GROUP, b3, r3, b_recv.at[q, c], piece(c))
 
         pick(pl.ds(pl.multiple_of(n * TILE, TILE), TILE), TILE)
-        for c in range(3):
+        for c in range(4):
 
             @pl.when(n == PIECES[c][1] - 1)
             def _(c=c):
-                if c == 2:
+                if c == 3:
                     pick(pl.ds(WIDE, EXTRA), EXTRA)
                 for i in (2, 1, 3):
                     o_copy(i, c).start()
@@ -367,7 +369,7 @@
         vg[0, lanes, :] = dot(left, rows_gu[:, :HID], (0, 0)).astype(BF)
         vu[0, lanes, :] = dot(left, rows_gu[:, HID:], (0, 0)).astype(BF)
 
-    for c in range(3):
+    for c in range(4):
         for i in (1, 2, 3):
             o_copy(i, c).wait_recv()
     for k in range(2):
@@ -379,7 +381,7 @@
 
     for i in (1, 2, 3):
         m_copy(i).wait_send()
-        for c in range(3):
+        for c in range(4):
             o_copy(i, c).wait_send()
     for a, (src, packed, dst) in enumerate(((x, px, xr), (g, pg, gr))):
         x_near(a, packed, dst).wait_send()
@@ -389,7 +391,7 @@
         count = GROUP - (q == 0)
         group_wait(count, 0, sx, x3, y_send.at[0, q])
         group_wait(count, 0, sg, g3, y_send.at[1, q])
-        for c in range(3):
+        for c in range(4):
             group_wait(count, 0, b3, r3, b_send.at[q, c], piece(c))
         d_copy(0, jnp.int32(q)).wait_send()
         d_copy(1, jnp.int32(q)).wait_send()
@@ -441,7 +443,7 @@
                 pltpu.VMEM((4, TOK, WIDE + EXTRA), BF),
                 pltpu.VMEM((4, TOK, WIDE + EXTRA), BF),
                 dma((3,)), dma((4,)), dma((4,)), dma((2, 4)), dma((2, 4)), dma((2, 4)), dma((2, 4)),
-                dma((2, 4)), dma((2, 4)), dma((4, 3)), dma((4, 3)), dma((4, 3)), dma((4, 3)),
+                dma((2, 4)), dma((2, 4)), dma((4, 4)), dma((4, 4)), dma((4, 4)), dma((4, 4)),
             ],
             compiler_params=pltpu.CompilerParams(
                 has_side_effects=True, collective_id=0, vmem_limit_bytes=49 << 20

time: 193 us -> 192 us (level)
  no operation moved by 1% of the time
where the time goes in v5:
time: 192 us
  Pallas kernels  191 us (99%)
    pallas_call x1, Pallas kernels, on_device(): pl.pallas_call(kernel, out_shape=(pltpu.VMEM((TOK, 2 * WIDE), BF), pltpu....  187 us
    pallas_call x1, Pallas kernels, on_device(): pl.pallas_call(place, out_shape=[jax.ShapeDtypeStruct(a.shape, a.dtype) f...  4.5 us

profile of v5, /device:TPU:0, one launch (start us, length us, event | category | flops | bytes accessed | tf_op | source)
XLA Modules:
  0.0 192.0 jit_solution(6369531387921379601)
XLA Ops:
  0.6 186.9 %shard_map.110 = (bf16[128,3584]{1,0:T(8,128)(2,1)S(1)}, bf16[1,128]{1,0:T(2,128)(2,1)S(1)}, bf16[1,1792,1024]{2,1,0:T(8,128)(2,1)S(1)}, bf16[1,1792,1024]{2,1,0:T(8,128)(2,1)S(1)}, bf16[1,1792,1024]{2,1,0:T(8,128)(2,1)S(1)}) custom-call(s32[1,128]{1,0:T(1,128)} %bitcast.3, bf16[1,128]{1,0:T(2,128)(2,1)} %bitcast.4, bf16[128,3584]{1,0:T(8,128)(2,1)} %x.1, ...), custom_call_target="tpu_custom_call" | custom-call | flops 22548578304 | bytes 22020096 | tf_op jit(solution)/shard_map/pallas_call | solution.py:418
  187.5 4.5 %shard_map.111 = (bf16[128,3584]{1,0:T(8,128)(2,1)}, bf16[1,128]{1,0:T(2,128)(2,1)}, bf16[1,1792,1024]{2,1,0:T(8,128)(2,1)}, bf16[1,1792,1024]{2,1,0:T(8,128)(2,1)}, bf16[1,1792,1024]{2,1,0:T(8,128)(2,1)}) custom-call(bf16[128,3584]{1,0:T(8,128)(2,1)S(1)} %get-tuple-element.15.refs_0_, bf16[1,128]{1,0:T(2,128)(2,1)S(1)} %get-tuple-element.16.refs_1_, ...), custom_call_target="tpu_custom_call" | custom-call | tf_op jit(solution)/shard_map/pallas_call | solution.py:461
